TPU v7x, 128 devices: a whole 4x4x4 slice. The times are simulated.
128 devices in a mesh: dp: 32 (over z, x, y_lo), blk: 4 (over y_hi, core).
Axes of the slice: x: 4, y: 4 (y_hi: 2, y_lo: 2; y = y_hi * 2 + y_lo), z: 4, core: 2. Of those that a mesh axis runs over, the one named last changes fastest.
Arguments:
- hidden: bfloat16 [32, 1536, 768], P('dp', 'blk'), may hold values from -6 to 6
- output_grad: bfloat16 [32, 1536, 768], P('dp', 'blk'), may hold values from -6 to 6
- block_counts: int32 [32], P('dp'), may hold values from 2 to 3, as said below
- slot_table: int32 [32, 3], P('dp'), may hold values from 0 to 2, as said below
- block_order_two: int32 [12, 2], replicated, may hold values from 0 to 1, each once within a row
- block_order_three: int32 [12, 3], replicated, may hold values from 0 to 2, each once within a row
- query_weight: bfloat16 [2, 768, 768], replicated, may hold values from -0.21875 to 0.21875
- key_weight: bfloat16 [2, 768, 768], replicated, may hold values from -0.21875 to 0.21875
- value_weight: bfloat16 [2, 768, 768], replicated, may hold values from -0.21875 to 0.21875
- output_weight: bfloat16 [2, 768, 768], replicated, may hold values from -3.5 to 3.5
- query_bias: bfloat16 [2, 768], replicated, may hold values from -2 to 2
- value_bias: bfloat16 [2, 768], replicated, may hold values from -2 to 2
- output_bias: bfloat16 [2, 768], replicated, may hold values from -2 to 2
- expand_weight: bfloat16 [2, 768, 3072], replicated, may hold values from -0.21875 to 0.21875
- expand_bias: bfloat16 [2, 3072], replicated, may hold values from -2 to 2
- reduce_weight: bfloat16 [2, 3072, 768], replicated, may hold values from -0.109375 to 0.109375
- reduce_bias: bfloat16 [2, 768], replicated, may hold values from -2 to 2
- first_gain: bfloat16 [2, 768], replicated, may hold values from 0.5 to 1.5
- first_shift: bfloat16 [2, 768], replicated, may hold values from -2 to 2
- second_gain: bfloat16 [2, 768], replicated, may hold values from 0.5 to 1.5
- second_shift: bfloat16 [2, 768], replicated, may hold values from -2 to 2
Outputs:
- activations: bfloat16 [32, 1536, 768], P('dp', 'blk')
- input_grad: bfloat16 [32, 1536, 768], P('dp', 'blk')
- grad_query_weight: float32 [2, 768, 768], P(None, ('dp', 'blk'))
- grad_key_weight: float32 [2, 768, 768], P(None, ('dp', 'blk'))
- grad_value_weight: float32 [2, 768, 768], P(None, ('dp', 'blk'))
- grad_output_weight: float32 [2, 768, 768], P(None, ('dp', 'blk'))
- grad_query_bias: float32 [2, 768], P(None, ('dp', 'blk'))
- grad_value_bias: float32 [2, 768], P(None, ('dp', 'blk'))
- grad_output_bias: float32 [2, 768], P(None, ('dp', 'blk'))
- grad_expand_weight: float32 [2, 768, 3072], P(None, ('dp', 'blk'))
- grad_expand_bias: float32 [2, 3072], P(None, ('dp', 'blk'))
- grad_reduce_weight: float32 [2, 3072, 768], P(None, ('dp', 'blk'))
- grad_reduce_bias: float32 [2, 768], P(None, ('dp', 'blk'))
- grad_first_gain: float32 [2, 768], P(None, ('dp', 'blk'))
- grad_first_shift: float32 [2, 768], P(None, ('dp', 'blk'))
- grad_second_gain: float32 [2, 768], P(None, ('dp', 'blk'))
- grad_second_shift: float32 [2, 768], P(None, ('dp', 'blk'))
Inputs may be any that keep to these rules, and one draw needn't show every extreme that they name: `block_counts`: blocks of each sequence; its remaining slots are padding. Each row is a permutation: slot_table[s, j] is the slot of block j of sequence s; where block_counts[s] = 2, block 2 sits in slot 1. `block_order_two`: each row is a permutation. `block_order_three`: each row is a permutation.
All inputs are finite; a program needn't handle non-finite values.
Results may differ from a plain program's by a relative error of at most 0.03.
Values may be sent and summed in bfloat16 or wider, within the bound.
A program may use at most 320 MiB of HBM per device.

v0:
```python
import functools

import jax
import jax.numpy as jnp
from jax import lax
from jax.experimental import pallas as pl
from jax.experimental.pallas import tpu as pltpu
from jax.sharding import Mesh
from jax.sharding import PartitionSpec as P

D = 768
FF = 3072
HEADS = 12
HD = 64
BLOCK = 512
SLOTS = 3
ROWS = 384
PIECE = 128
CHUNK = 768
HALF = 384
BLK = ("blk_0", "blk_1")
DP_BLK = ("dp_0", "dp_1", "dp_2", "blk_0", "blk_1")
DP = ("dp_0", "dp_1", "dp_2")
EPSILON = 1e-06
ROOT_HALF = 0.7071067811865476
INV_ROOT_TAU = 0.3989422804014327
SCALE = HD ** (-0.5)
MESH = pl.DeviceIdType.MESH
BF = jnp.bfloat16
F32 = jnp.float32
MIB = 1024 * 1024
VMEM = pl.BlockSpec(memory_space=pltpu.VMEM)
SMEM = pl.BlockSpec(memory_space=pltpu.SMEM)
ANY = pl.BlockSpec(memory_space=pl.ANY)


def dot(left, right):
    return jnp.dot(left, right, preferred_element_type=F32)


def dot_nt(left, right):
    return lax.dot_general(left, right, (((1,), (1,)), ((), ())), preferred_element_type=F32)


def dot_tn(left, right):
    return lax.dot_general(left, right, (((0,), (0,)), ((), ())), preferred_element_type=F32)


def params(limit=60):
    return pltpu.CompilerParams(vmem_limit_bytes=limit * MIB)


def row_of(ref, layer):
    return ref[layer : layer + 1, :].astype(F32)


def norm_parts(residual):
    mean = jnp.mean(residual, axis=-1, keepdims=True)
    centred = residual - mean
    inv_std = lax.rsqrt(jnp.mean(centred * centred, axis=-1, keepdims=True) + EPSILON)
    return centred * inv_std, inv_std


def norm_backward(grad, gain, normed, inv_std):
    scaled = grad * gain
    return inv_std * (
        scaled
        - jnp.mean(scaled, axis=-1, keepdims=True)
        - normed * jnp.mean(scaled * normed, axis=-1, keepdims=True)
    )


def layer_block(layer, shape, index):
    return pl.BlockSpec((None,) + shape, lambda j: (layer,) + index(j))


def peer_of(axis, place, offset):
    at = lax.rem(place[axis] + offset, 4)
    if axis == 0:
        return {"dp_0": at}
    if axis == 1:
        return {"dp_1": at}
    return {"dp_2": lax.rem(at, 2), "blk_0": at // 2}


def pos_device(t):
    return {"dp_2": t // 4, "blk_0": lax.rem(t // 2, 2), "blk_1": lax.rem(t, 2)}


def columns_at(start, count):
    return pl.ds(pl.multiple_of(start, 128), count)


STREAM_ORDERS = ((2, 0, 1), (1, 2, 0), (0, 1, 2))
LAYOUT = {"q": (2, 0, 1), "e": (2, 0, 1), "r": (0, 1, 2)}
PIECES = (48, 128)
LEFT = ((4, 4) + PIECES, (4,) + PIECES, PIECES)
WHOLE = (3, 4) + LEFT[0]


def share(group, stage, stream, ref, at):
    order, left = STREAM_ORDERS[stream], list(LAYOUT[group])
    for done in order[:stage]:
        left.remove(done)
    if group == "r" and order[stage] == 2:
        at = lax.rem(at, 2) * 2 + at // 2
    index = [slice(None)] * left.index(order[stage]) + [at]
    return ref.at[(stream, *index)]


def add_up(own, got, out, streams=3):
    count = out.shape[1] * out.shape[2] if len(out.shape) == 5 else out.shape[1]
    for n in range(streams):

        @pl.loop(0, count)
        def _(k, n=n):
            at = (k // 4, lax.rem(k, 4)) if len(out.shape) == 5 else (k,)
            total = own[n](at).astype(F32)
            for d in range(3):
                total += got[(n, d) + at].astype(F32)
            out[(n,) + at] = total.astype(out.dtype)


def chip_place():
    y = lax.axis_index("blk_0") * 2 + lax.axis_index("dp_2")
    return (lax.axis_index("dp_0"), lax.axis_index("dp_1"), y)


def stage_copies(group, stage, source, got, send, recv):
    place = chip_place()
    copies = []
    for d in (2, 1, 3):
        for n in range(3):
            axis = STREAM_ORDERS[n][stage]
            src = share(group, stage, n, source, lax.rem(place[axis] + d, 4))
            copies.append(remote(src, got.at[n, d - 1], send.at[n, d - 1], recv.at[n, d - 1], peer_of(axis, place, d)))
    return copies


def own_share(group, stage, stream, source):
    return share(group, stage, stream, source, chip_place()[STREAM_ORDERS[stream][stage]])


def own_loads(group, stage, source, held, got, got_held, sems):
    out = [pltpu.make_async_copy(own_share(group, stage, n, source), held.at[n], sems.at[n]) for n in range(3)]
    return out + [pltpu.make_async_copy(got, got_held, sems.at[3])]


def add_held(held, got, out):
    add_up([lambda at, n=n: held[(n,) + at] for n in range(3)], got, out)


def add_direct(group, stage, source, got, out):
    views = [own_share(group, stage, n, source) for n in range(3)]
    add_up([lambda at, v=v: v[at] for v in views], got, out)


def axis_peers(axes, offsets=(1, 2, 3)):
    place = chip_place()
    return [peer_of(a, place, d) for a in axes for d in offsets]


def landing(stage):
    return jax.ShapeDtypeStruct((3, 3) + LEFT[stage], BF)


def summed(stage):
    return (3,) + LEFT[stage]


def begin(copies):
    for c in copies:
        c.start()
    return copies


def end(copies):
    for c in copies:
        c.wait()


class Late:
    def __init__(self, source, held, sem):
        self.copy, self.held, self.waited = pltpu.make_async_copy(source, held, sem), held, False
        self.copy.start()

    def __call__(self):
        if not self.waited:
            self.copy.wait()
            self.waited = True
        return self.held


def pieces_of(grad):
    return [grad[:, k * 128 : (k + 1) * 128].reshape(4, 4, 48, 128) for k in range(3)]


def places():
    y_hi, core = lax.axis_index("blk_0"), lax.axis_index("blk_1")
    return y_hi, core, y_hi * 2 + core


def remote(src, dst, send, recv, device):
    return pltpu.make_async_remote_copy(
        src_ref=src, dst_ref=dst, send_sem=send, recv_sem=recv, device_id=device, device_id_type=MESH
    )


def rows_at(start, count):
    return pl.ds(pl.multiple_of(start, PIECE), count)


def greet(devices):
    barrier = pltpu.get_barrier_semaphore()
    for device in devices:
        pl.semaphore_signal(barrier, inc=1, device_id=device, device_id_type=MESH)
    pl.semaphore_wait(barrier, len(devices))


FAR = (256, ROWS)


def far_plan(layer, y_hi, core, block):
    if layer == 0:
        partner = {"blk_0": 1 - y_hi, "blk_1": 1 - core}
        return partner, jnp.where(block == 1, 128, 0), jnp.where(block == 1, 768, 512)
    return {"blk_0": 1 - y_hi}, 0, lax.rem(block + 2, 4) * ROWS


def is_middle(block):
    return jnp.logical_and(block >= 1, block <= 2)


def project_kernel(
    layer, h, wq, wk, wv, bq, bv, q, kv_all, rows_all, low, kv, far, kv_far, held_q, held_k, held_v, late, local, send, recv
):
    wk, wv = Late(wk.at[layer], held_k, late.at[0]), Late(wv.at[layer], held_v, late.at[1])
    wq = Late(wq.at[layer], held_q, late.at[2])
    y_hi, core, block = places()
    far_rows = FAR[layer]
    sibling = {"blk_1": 1 - core}
    partner, give, theirs = far_plan(layer, y_hi, core, block)
    low[...] = h[...].astype(BF)
    greet([sibling, partner])
    hidden = remote(low.at[rows_at(give, far_rows)], far, send.at[0], recv.at[0], partner)

    def talk(step):
        if layer == 0:
            pl.when(is_middle(block))(step)
        else:
            step()

    def both(src, dst, n):
        return [remote(src, dst, send.at[n], recv.at[n], sibling), pltpu.make_async_copy(src, dst, local.at[n])]

    talk(lambda: hidden.start())
    copies = both(low, rows_all.at[core, pl.ds(0, ROWS)], 1)
    kv[0] = dot(low[...], wk()[...]).astype(BF)
    kv[1] = (dot(low[...], wv()[...]) + row_of(bv, layer)).astype(BF)
    copies += both(kv, kv_all.at[:, rows_at(block * ROWS, ROWS)], 2)
    for c in copies:
        c.start()
    q[...] = (dot(low[...], wq()[...]) + row_of(bq, layer)).astype(BF)
    far_place = kv_all.at[:, rows_at(theirs, far_rows)]
    keep_far = pltpu.make_async_copy(kv_far, far_place, local.at[3])

    def far_keys():
        kv_far[0] = dot(far[...], wk()[...]).astype(BF)
        kv_far[1] = (dot(far[...], wv()[...]) + row_of(bv, layer)).astype(BF)
        keep_far.start()

    talk(lambda: hidden.wait())
    if layer == 0:

        @pl.when(jnp.logical_not(is_middle(block)))
        def _():
            far[...] = jnp.zeros_like(far)

    last = both(far, rows_all.at[core, pl.ds(ROWS, far_rows)], 4)
    for c in last:
        c.start()
    talk(far_keys)
    if layer == 1:
        relay = remote(kv_far, far_place, send.at[3], recv.at[3], sibling)
        relay.start()
        relay.wait()
    talk(lambda: keep_far.wait())
    for c in copies + last:
        c.wait()


def project(layer, h, w):
    shape, dma, far_rows = jax.ShapeDtypeStruct, pltpu.SemaphoreType.DMA, FAR[layer]
    q, kv_all, rows_all = pl.pallas_call(
        functools.partial(project_kernel, layer),
        out_shape=(shape((ROWS, D), BF), shape((2, SLOTS * BLOCK, D), BF), shape((2, ROWS + far_rows, D), BF)),
        in_specs=[VMEM, ANY, ANY, ANY, VMEM, VMEM],
        out_specs=(VMEM, ANY, ANY),
        scratch_shapes=[
            pltpu.VMEM((ROWS, D), BF), pltpu.VMEM((2, ROWS, D), BF), pltpu.VMEM((far_rows, D), BF),
            pltpu.VMEM((2, far_rows, D), BF), pltpu.VMEM((D, D), BF), pltpu.VMEM((D, D), BF), pltpu.VMEM((D, D), BF), dma((3,)),
            dma((5,)), dma((5,)), dma((5,)),
        ],
        compiler_params=pltpu.CompilerParams(collective_id=1 + layer, has_side_effects=True, vmem_limit_bytes=60 * MIB),
        name=f"project_{layer}",
    )(h, w["query_weight"], w["key_weight"], w["value_weight"], w["query_bias"], w["value_bias"])
    return q, kv_all.reshape(2, SLOTS, BLOCK, D), rows_all


def project_back_body(layer, rows, gq, parts, gres, dwo, wq, wk, wv, p0, gh, scratch, peers, hooks):
    (
        grads, near, far_near, gh_send, gh_got, qcat, kvcat, local, send, recv,
        held_rows, held_gq, held_gres, held_dwo, held_q, held_k, held_v, late,
    ) = scratch
    y_hi, core, block = places()
    far_rows = FAR[layer]
    sibling = {"blk_1": 1 - core}
    partner, give, theirs = far_plan(layer, y_hi, core, block)
    mine = columns_at(core * HALF, HALF)
    yours = columns_at((1 - core) * HALF, HALF)

    def hook(name):
        if name in hooks:
            hooks[name]()

    def talk(step):
        if layer == 0:
            pl.when(is_middle(block))(step)
        else:
            step()

    own = begin(
        [
            pltpu.make_async_copy(parts.at[:, rows_at(theirs, far_rows)], grads.at[:, pl.ds(ROWS, far_rows)], local.at[0]),
            pltpu.make_async_copy(parts.at[:, rows_at(block * ROWS, ROWS)], grads.at[:, pl.ds(0, ROWS)], local.at[1]),
            pltpu.make_async_copy(gq.at[:, mine], qcat.at[core], local.at[2]),
        ]
    )
    wk, wv = Late(wk.at[layer], held_k, late.at[0]), Late(wv.at[layer], held_v, late.at[1])
    dwo, rows = Late(dwo, held_dwo, late.at[2]), Late(rows, held_rows, late.at[3])
    gq_held, wq = Late(gq, held_gq, late.at[4]), Late(wq.at[layer], held_q, late.at[5])
    gres = Late(gres, held_gres, late.at[6])
    hook("loads")
    greet(peers or [sibling, partner] + axis_peers((0, 1, 2), (1, 2, 3)))
    beside = y_hi * 2 + 1 - core
    copies = []
    if layer == 1:
        at = (1 - y_hi) * 2 + 1 - core
        copies.append(remote(parts.at[:, rows_at(at * ROWS, ROWS)], far_near, send.at[0], recv.at[0], sibling))
    copies.append(remote(parts.at[:, rows_at(beside * ROWS, ROWS)], near, send.at[1], recv.at[1], sibling))
    half_q = remote(gq.at[:, yours], qcat.at[core], send.at[3], recv.at[3], sibling)
    begin(copies + [half_q])
    hook("greeted")

    def place_square(y, grad):
        for k, piece in enumerate(pieces_of(grad)):
            p0[k, y] = piece

    own[0].wait()
    wk(), wv()
    if layer == 1:
        copies[0].wait()
        grads[:, ROWS:] = (grads[:, ROWS:].astype(F32) + far_near[...].astype(F32)).astype(BF)
    hidden = remote(gh_send, gh_got, send.at[2], recv.at[2], partner)

    def far_part():
        gh_send[...] = (dot_nt(grads[0, ROWS:], wk()[...]) + dot_nt(grads[1, ROWS:], wv()[...])).astype(BF)
        hidden.start()

    talk(far_part)
    hook("far")
    own[1].wait()
    copies[-1].wait()
    grads[:, 0:ROWS] = (grads[:, 0:ROWS].astype(F32) + near[...].astype(F32)).astype(BF)
    half_kv = remote(grads.at[:, :, yours], kvcat.at[:, core], send.at[4], recv.at[4], sibling)
    half_kv.start()
    kvcat[:, core] = grads[:, :, mine]
    hook("near")
    place_square(1, dwo()[...])
    own[2].wait()
    half_q.wait()
    rows = rows()
    place_square(0, (dot_tn(rows[0, 0:ROWS], qcat[0]) + dot_tn(rows[1, 0:ROWS], qcat[1])).astype(BF))
    hook("two_squares")
    half_kv.wait()
    for side in (0, 1):
        cat = kvcat[side].reshape(2 * (ROWS + far_rows), HALF)
        place_square(2 + side, dot_tn(rows[...].reshape(2 * (ROWS + far_rows), D), cat).astype(BF))
    hook("squares")
    total = gres()[...] + dot_nt(gq_held()[...], wq()[...])
    total += dot_nt(grads[0, 0:ROWS], wk()[...]) + dot_nt(grads[1, 0:ROWS], wv()[...])
    if layer == 1:
        hidden.wait()
        gh[...] = (total + gh_got[...].astype(F32)).astype(gh.dtype)
    else:
        gh[...] = total.astype(gh.dtype)

        @pl.when(is_middle(block))
        def _():
            hidden.wait()
            here = rows_at(give, far_rows)
            gh[here, :] = (gh[here, :].astype(F32) + gh_got[...].astype(F32)).astype(gh.dtype)


def project_back_scratch(layer):
    far_rows, dma = FAR[layer], pltpu.SemaphoreType.DMA
    return [
        pltpu.VMEM((2, ROWS + far_rows, D), BF), pltpu.VMEM((2, ROWS, D), BF),
        pltpu.VMEM((2, far_rows, D), BF), pltpu.VMEM((far_rows, D), BF), pltpu.VMEM((far_rows, D), BF),
        pltpu.VMEM((2, ROWS, HALF), BF), pltpu.VMEM((2, 2, ROWS + far_rows, HALF), BF),
        dma((3,)), dma((5,)), dma((5,)),
        pltpu.VMEM((2, ROWS + far_rows, D), BF), pltpu.VMEM((ROWS, D), BF), pltpu.VMEM((ROWS, D), F32), pltpu.VMEM((D, HALF), BF),
        pltpu.VMEM((D, D), BF), pltpu.VMEM((D, D), BF), pltpu.VMEM((D, D), BF), dma((7,)),
    ]


def own_scratch(stage):
    return pltpu.VMEM(summed(stage), BF)


def got_scratch(stage):
    return pltpu.VMEM((3, 3) + LEFT[stage], BF)


def project_back_two_kernel(
    rows, gq, parts, gres, dwo, wq, wk, wv, low_all, gi, gi_other, r0, got_r0, p0_out, gh, e_out, s_r, got_r, *refs
):
    scratch, (p0, e, gicat, held_low, own_r, held_r, csems, gsems, osems, csend, crecv) = refs[:18], refs[18:]
    core = lax.axis_index("blk_1")
    loads_g, loads_r, carried = [], [], []

    def loads():
        loads_r.extend(begin(own_loads("r", 0, r0, own_r, got_r0, held_r, csems)))
        loads_g.extend(
            begin(
                [
                    pltpu.make_async_copy(gi.at[core], gicat.at[core], gsems.at[0]),
                    pltpu.make_async_copy(gi_other, gicat.at[1 - core], gsems.at[1]),
                    pltpu.make_async_copy(low_all, held_low, gsems.at[2]),
                ]
            )
        )

    def two_squares():
        end(loads_r)
        add_held(own_r, held_r, s_r)
        carried.extend(begin(stage_copies("r", 1, s_r, got_r, csend, crecv)))
        end(loads_g)
        for y in (0, 2):
            both = gicat[:, :, y * HALF : (y + 2) * HALF].reshape(2 * ROWS, 2 * HALF)
            grad = dot_tn(held_low[...].reshape(2 * ROWS, D), both).astype(BF)
            for k, piece in enumerate(pieces_of(grad[:, :HALF])):
                e[k, y] = piece
            for k, piece in enumerate(pieces_of(grad[:, HALF:])):
                e[k, y + 1] = piece
        carried.extend(begin([pltpu.make_async_copy(e, e_out, osems.at[0])]))

    def squares():
        carried.extend(begin([pltpu.make_async_copy(p0, p0_out, osems.at[1])]))

    hooks = dict(loads=loads, two_squares=two_squares, squares=squares)
    project_back_body(1, rows, gq, parts, gres, dwo, wq, wk, wv, p0, gh, scratch, None, hooks)
    end(carried)


def project_back_two(rows_all, gq, parts, gres, dwo, w, low_all, carry):
    shape, dma = jax.ShapeDtypeStruct, pltpu.SemaphoreType.DMA
    return pl.pallas_call(
        project_back_two_kernel,
        out_shape=(shape(WHOLE, BF), shape((ROWS, D), F32), shape(WHOLE, BF), shape(summed(0), BF), landing(1)),
        in_specs=[ANY] * 13,
        out_specs=(ANY, VMEM, ANY, VMEM, ANY),
        scratch_shapes=project_back_scratch(1)
        + [pltpu.VMEM(WHOLE, BF), pltpu.VMEM(WHOLE, BF), pltpu.VMEM((2, ROWS, STEPS * HALF), BF), pltpu.VMEM((2, ROWS, D), BF)]
        + [own_scratch(0), got_scratch(0), dma((4,)), dma((3,)), dma((2,)), dma((3, 3)), dma((3, 3))],
        compiler_params=pltpu.CompilerParams(collective_id=4, has_side_effects=True, vmem_limit_bytes=60 * MIB),
        name="project_back_1",
    )(rows_all, gq, parts.reshape(2, SLOTS * BLOCK, D), gres, dwo, w["query_weight"], w["key_weight"], w["value_weight"],
      low_all, *carry)


def slots_of(layer, tab, cnt, two, three, piece, head):
    block = lax.axis_index("blk_0") * 2 + lax.axis_index("blk_1")
    t = (3 * block + piece) // 4
    j = jnp.where(tab[0, 1] == t, 1, jnp.where(tab[0, 2] == t, 2, 0))
    live = jnp.where(j < cnt[0], 1.0, 0.0)
    if layer == 0:
        return t, live
    from_two = jnp.where(j < 2, two[head, jnp.minimum(j, 1)], j)
    chosen = jnp.where(cnt[0] == SLOTS, three[head, j], from_two)
    return tab[0, chosen], live


def left_lanes(rows=1):
    return lax.broadcasted_iota(jnp.int32, (rows, 2 * HD), 1) < HD


def two_heads(tile):
    left, none = left_lanes(PIECE), jnp.zeros_like(tile)
    return jnp.concatenate([jnp.where(left, tile, none), jnp.where(left, none, tile)], axis=0)


def own_columns(both):
    return jnp.where(left_lanes(PIECE), both[:PIECE], both[PIECE:])


def slot_mask(s0, s1, t, kind):
    first, second = jnp.where(s0 == t, 1.0, 0.0), jnp.where(s1 == t, 1.0, 0.0)
    return jnp.where(left_lanes(), first, second).astype(kind)


def soft(scores):
    top = jnp.max(scores, axis=0, keepdims=True)
    e = jnp.exp((scores - top) * SCALE)
    return e * (1.0 / jnp.sum(e, axis=0, keepdims=True))


def attend_kernel(layer, tab, cnt, two, three, q, k, v, mixed):
    pair = pl.program_id(0)
    left = left_lanes(BLOCK)
    for i in range(3):
        rows = pl.ds(i * PIECE, PIECE)
        s0, live = slots_of(layer, tab, cnt, two, three, i, 2 * pair)
        if layer == 0:
            keys, values = k[s0], v[s0]
        else:
            s1, _ = slots_of(layer, tab, cnt, two, three, i, 2 * pair + 1)
            keys, values = jnp.where(left, k[s0], k[s1]), jnp.where(left, v[s0], v[s1])
        weights = soft(dot_nt(keys, two_heads(q[rows, :]))).astype(BF)
        mixed[rows, :] = (own_columns(dot_tn(weights, values)) * live).astype(BF)


def attend_specs():
    tile = pl.BlockSpec((ROWS, 2 * HD), lambda p: (0, p))
    keys = pl.BlockSpec((None, SLOTS, BLOCK, 2 * HD), lambda p: (0, 0, 0, p))
    values = pl.BlockSpec((None, SLOTS, BLOCK, 2 * HD), lambda p: (1, 0, 0, p))
    return tile, keys, values


def attend(layer, table, q, kv_all):
    tile, keys, values = attend_specs()
    return pl.pallas_call(
        functools.partial(attend_kernel, layer),
        grid=(HEADS // 2,),
        out_shape=jax.ShapeDtypeStruct((ROWS, D), BF),
        in_specs=[SMEM] * 4 + [tile, keys, values],
        out_specs=tile,
        compiler_params=params(),
        name=f"attend_{layer}",
    )(*table, q, kv_all, kv_all)


def attend_back_step(layer, tab, cnt, two, three, q, k, v, gm, gq, gkv, acc):
    pair = pl.program_id(0)
    masks = []
    if layer == 0:
        acc[...] = jnp.zeros_like(acc)
    for i in range(3):
        rows = pl.ds(i * PIECE, PIECE)
        s0, live = slots_of(layer, tab, cnt, two, three, i, 2 * pair)
        if layer == 0:
            keys, values = k[s0], v[s0]
        else:
            s1, _ = slots_of(layer, tab, cnt, two, three, i, 2 * pair + 1)
            low = [slot_mask(s0, s1, t, BF) for t in range(SLOTS)]
            masks.append([slot_mask(s0, s1, t, F32) for t in range(SLOTS)])
            keys = k[0] * low[0] + k[1] * low[1] + k[2] * low[2]
            values = v[0] * low[0] + v[1] * low[1] + v[2] * low[2]
        qq = two_heads(q[rows, :])
        gg = two_heads((gm[rows, :].astype(F32) * live).astype(BF))
        weights = soft(dot_nt(keys, qq))
        grad_weights = dot_nt(values, gg)
        delta = jnp.sum(weights * grad_weights, axis=0, keepdims=True)
        grad_scores = (weights * (grad_weights - delta)).astype(BF)
        gq[rows, :] = (own_columns(dot_tn(grad_scores, keys)) * SCALE).astype(BF)
        gk = dot(grad_scores, qq) * SCALE
        gv = dot(weights.astype(BF), gg)
        if layer == 0:
            acc[0, s0] += gk
            acc[1, s0] += gv
        else:
            acc[0, i] = gk
            acc[1, i] = gv
    if layer == 0:
        gkv[...] = acc[...].astype(BF)
    else:
        for side in range(2):
            for t in range(SLOTS):
                total = acc[side, 0] * masks[0][t] + acc[side, 1] * masks[1][t] + acc[side, 2] * masks[2][t]
                gkv[side, t] = total.astype(BF)


def attend_back_kernel(layer, tab, cnt, two, three, q, k, v, gm, e, r, gq, gkv, vec, got_e, got_r, acc, send, recv):
    step = pl.program_id(0)
    core = lax.axis_index("blk_1")

    def carried():
        copies = stage_copies("r", 0, r, got_r, send.at[0], recv.at[0])
        if layer == 0:
            return copies + stage_copies("e", 0, e, got_e, send.at[1], recv.at[1])
        return copies + [remote(e.at[1 - core], got_e, send.at[1, 0, 0], recv.at[1, 0, 0], {"blk_1": 1 - core})]

    peers = axis_peers((0, 1, 2)) + ([{"blk_1": 1 - core}] if layer == 1 else [])

    @pl.when(step == 0)
    def _():
        barrier = pltpu.get_barrier_semaphore()
        for peer in peers:
            pl.semaphore_signal(barrier, inc=1, device_id=peer, device_id_type=MESH)

    attend_back_step(layer, tab, cnt, two, three, q, k, v, gm, gq, gkv, acc)
    vec[0:1] = jnp.sum(gq[...].astype(F32), axis=0, keepdims=True)
    total = jnp.zeros((1, 2 * HD), F32)
    for i in range(3):
        _, live = slots_of(0, tab, cnt, two, three, i, 0)
        total += live * jnp.sum(gm[i * PIECE : (i + 1) * PIECE, :].astype(F32), axis=0, keepdims=True)
    vec[1:2] = total

    @pl.when(step == 0)
    def _():
        pl.semaphore_wait(pltpu.get_barrier_semaphore(), len(peers))
        begin(carried())

    @pl.when(step == HEADS // 2 - 1)
    def _():
        end(carried())


def attend_back(layer, table, q, kv_all, gm, e, r):
    tile, keys, values = attend_specs()
    both = pl.BlockSpec((2, SLOTS, BLOCK, 2 * HD), lambda p: (0, 0, 0, p))
    shape, dma = jax.ShapeDtypeStruct, pltpu.SemaphoreType.DMA
    landed = landing(0) if layer == 0 else shape((ROWS, STEPS * HALF), BF)
    return pl.pallas_call(
        functools.partial(attend_back_kernel, layer),
        grid=(HEADS // 2,),
        out_shape=(shape((ROWS, D), BF), shape((2, SLOTS, BLOCK, D), BF), shape((2, D), F32), landed, landing(0)),
        in_specs=[SMEM] * 4 + [tile, keys, values, tile, ANY, ANY],
        out_specs=(tile, both, pl.BlockSpec((2, 2 * HD), lambda p: (0, p)), ANY, ANY),
        scratch_shapes=[pltpu.VMEM((2, SLOTS, BLOCK, 2 * HD), F32), dma((2, 3, 3)), dma((2, 3, 3))],
        compiler_params=pltpu.CompilerParams(collective_id=9 + layer, has_side_effects=True, vmem_limit_bytes=60 * MIB),
        name=f"attend_back_{layer}",
    )(*table, q, kv_all, kv_all, gm, e, r)


STEPS = FF // CHUNK


def tail_kernel(
    layer, mixed, h, wo, bo, g1, s1, we, be, wr, br, g2, s2, r1, r2, out, slope, act_all, low_all, mixed_all,
    first, total, low, act, local, send, recv,
):
    j = pl.program_id(0)
    core = lax.axis_index("blk_1")
    sibling = {"blk_1": 1 - core}

    def both(src, dst, n):
        return [remote(src, dst, send.at[n], recv.at[n], sibling), pltpu.make_async_copy(src, dst, local.at[n])]

    def act_copies(at):
        return both(act.at[at], act_all.at[core, :, columns_at(at * CHUNK, CHUNK)], at)

    early = both(mixed, mixed_all.at[core], STEPS) + both(low, low_all.at[core], STEPS + 1)

    @pl.when(j == 0)
    def _():
        barrier = pltpu.get_barrier_semaphore()
        pl.semaphore_signal(barrier, inc=1, device_id=sibling, device_id_type=MESH)
        residual = h[...].astype(F32) + dot(mixed[...], wo[...]) + row_of(bo, layer)
        r1[...] = residual
        normed, _ = norm_parts(residual)
        first[...] = normed * row_of(g1, layer) + row_of(s1, layer)
        low[...] = first[...].astype(BF)
        total[...] = jnp.zeros_like(total)
        pl.semaphore_wait(barrier, 1)
        for c in early:
            c.start()

    inner = dot(low[...], we[...]) + be[layer : layer + 1, columns_at(j * CHUNK, CHUNK)].astype(F32)
    phi = 0.5 * (1.0 + lax.erf(inner * ROOT_HALF))
    low_act = (inner * phi).astype(BF)
    act[j] = low_act
    for c in act_copies(j):
        c.start()
    slope[...] = (phi + inner * (INV_ROOT_TAU * jnp.exp(-0.5 * inner * inner))).astype(BF)
    total[...] += dot(low_act, wr[...])

    @pl.when(j == STEPS - 1)
    def _():
        residual = first[...] + total[...] + row_of(br, layer)
        r2[...] = residual
        normed, _ = norm_parts(residual)
        out[...] = (normed * row_of(g2, layer) + row_of(s2, layer)).astype(out.dtype)
        for c in early:
            c.wait()
        for at in range(STEPS):
            for c in act_copies(at):
                c.wait()


def tail(layer, mixed, h, w, out_type):
    square = layer_block(layer, (D, D), lambda j: (0, 0))
    wide = layer_block(layer, (D, CHUNK), lambda j: (0, j))
    tall = layer_block(layer, (CHUNK, D), lambda j: (j, 0))
    full = pl.BlockSpec((ROWS, D), lambda j: (0, 0))
    vec, dma = VMEM, pltpu.SemaphoreType.DMA
    shape = jax.ShapeDtypeStruct
    return pl.pallas_call(
        functools.partial(tail_kernel, layer),
        grid=(STEPS,),
        out_shape=(
            shape((ROWS, D), F32), shape((ROWS, D), F32), shape((ROWS, D), out_type), shape((ROWS, FF), BF),
            shape((2, ROWS, FF), BF), shape((2, ROWS, D), BF), shape((2, ROWS, D), BF),
        ),
        in_specs=[full, full, square, vec, vec, vec, wide, vec, tall, vec, vec, vec],
        out_specs=(full, full, full, pl.BlockSpec((ROWS, CHUNK), lambda j: (0, j)), ANY, ANY, ANY),
        scratch_shapes=[
            pltpu.VMEM((ROWS, D), F32), pltpu.VMEM((ROWS, D), F32), pltpu.VMEM((ROWS, D), BF),
            pltpu.VMEM((STEPS, ROWS, CHUNK), BF), dma((STEPS + 2,)), dma((STEPS + 2,)), dma((STEPS + 2,)),
        ],
        compiler_params=pltpu.CompilerParams(collective_id=5 + layer, has_side_effects=True, vmem_limit_bytes=60 * MIB),
        name=f"tail_{layer}",
    )(mixed, h, w["output_weight"], w["output_bias"], w["first_gain"], w["first_shift"], w["expand_weight"], w["expand_bias"],
      w["reduce_weight"], w["reduce_bias"], w["second_gain"], w["second_shift"])


def tail_back_kernel(layer, g, r1, r2, low_all, act_all, slope, mixed_all, wo, we, wr, g1, g2, *refs):
    refs = list(refs)

    def take(count):
        out, refs[:count] = refs[:count], []
        return out

    q_in, e_in = take(2) if layer == 0 else (None, None)
    dwr, dwe, dwo, gres, gm, vec, vec_e = take(7)
    got_q, got_e = take(2) if layer == 0 else (None, None)
    go, ga, gi, total, gocat, gacat, gicat, send, recv = take(9)
    last = STEPS if layer == 0 else STEPS - 1

    def carried():
        if layer == 1:
            return []
        csend, crecv = refs
        return stage_copies("q", 0, q_in, got_q, csend.at[0], crecv.at[0]) + stage_copies(
            "e", 0, e_in, got_e, csend.at[1], crecv.at[1]
        )

    j = pl.program_id(0)
    core = lax.axis_index("blk_1")
    sibling = {"blk_1": 1 - core}
    mine, yours = columns_at(core * HALF, HALF), columns_at((1 - core) * HALF, HALF)

    def share_go():
        return remote(go.at[:, yours], gocat.at[core], send.at[STEPS], recv.at[STEPS], sibling)

    def share_ga():
        return remote(ga.at[:, yours], gacat.at[core], send.at[STEPS + 1], recv.at[STEPS + 1], sibling)

    def share_gi(at):
        return remote(gi.at[at, :, yours], gicat.at[at, core], send.at[at], recv.at[at], sibling)

    @pl.when(j == 0)
    def _():
        barrier = pltpu.get_barrier_semaphore()
        peers = [sibling] + (axis_peers((0, 1, 2)) if layer == 0 else [])
        for peer in peers:
            pl.semaphore_signal(barrier, inc=1, device_id=peer, device_id_type=MESH)
        grad = g[...].astype(F32)
        normed, inv_std = norm_parts(r2[...])
        grad_r = norm_backward(grad, row_of(g2, layer), normed, inv_std)
        vec[0:1] = jnp.sum(grad * normed, axis=0, keepdims=True)
        vec[1:2] = jnp.sum(grad, axis=0, keepdims=True)
        total[...] = grad_r
        go[...] = grad_r.astype(BF)
        vec[2:3] = jnp.sum(go[...].astype(F32), axis=0, keepdims=True)
        pl.semaphore_wait(barrier, len(peers))
        share_go().start()
        begin(carried())
        gocat[core] = go[:, mine]

    @pl.when(j < STEPS)
    def _():
        grad_inner = (dot_nt(go[...], wr[...]) * slope[...].astype(F32)).astype(BF)
        if layer == 0:
            gi[j] = grad_inner
            share_gi(j).start()
            gicat[j, core] = gi[j, :, mine]
        else:
            dwe[0], dwe[1] = grad_inner[:, :HALF], grad_inner[:, HALF:]
        vec_e[...] = jnp.sum(grad_inner.astype(F32), axis=0, keepdims=True)
        total[...] += dot_nt(grad_inner, we[...])

        @pl.when(j == 0)
        def _():
            share_go().wait()

        grad = dot_tn(act_all[...].reshape(2 * ROWS, CHUNK), gocat[...].reshape(2 * ROWS, HALF)).astype(BF)
        for k, piece in enumerate(pieces_of(grad)):
            dwr[k, 0] = piece

    @pl.when(j == STEPS - 1)
    def _():
        grad = total[...]
        normed, inv_std = norm_parts(r1[...])
        grad_r = norm_backward(grad, row_of(g1, layer), normed, inv_std)
        vec[3:4] = jnp.sum(grad * normed, axis=0, keepdims=True)
        vec[4:5] = jnp.sum(grad, axis=0, keepdims=True)
        gres[...] = grad_r
        ga[...] = grad_r.astype(BF)
        vec[5:6] = jnp.sum(ga[...].astype(F32), axis=0, keepdims=True)
        share_ga().start()
        gacat[core] = ga[:, mine]

    if layer == 0:

        @pl.when(j > 0)
        def _():
            share_gi(j - 1).wait()
            grad = dot_tn(low_all[...].reshape(2 * ROWS, D), gicat[j - 1].reshape(2 * ROWS, HALF)).astype(BF)
            for k, piece in enumerate(pieces_of(grad)):
                dwe[k, 0] = piece

    @pl.when(j == last)
    def _():
        gm[...] = dot_nt(ga[...], wo[...]).astype(BF)
        share_ga().wait()
        dwo[...] = dot_tn(mixed_all[...].reshape(2 * ROWS, D), gacat[...].reshape(2 * ROWS, HALF)).astype(BF)
        end(carried())


def tail_back(layer, g, saved, w, carry=()):
    at = lambda j: jnp.minimum(j, STEPS - 1)
    square = layer_block(layer, (D, D), lambda j: (0, 0))
    wide = layer_block(layer, (D, CHUNK), lambda j: (0, at(j)))
    tall = layer_block(layer, (CHUNK, D), lambda j: (at(j), 0))
    full = pl.BlockSpec((ROWS, D), lambda j: (0, 0))
    pair = pl.BlockSpec((2, ROWS, D), lambda j: (0, 0, 0))
    vec, dma = VMEM, pltpu.SemaphoreType.DMA
    shape = jax.ShapeDtypeStruct
    chunk = pl.BlockSpec((3, 1) + LEFT[0], lambda j: (0, at(j), 0, 0, 0, 0))
    if layer == 0:
        expand, expand_spec = shape(WHOLE, BF), pl.BlockSpec((3, 1) + LEFT[0], lambda j: (0, jnp.maximum(j - 1, 0), 0, 0, 0, 0))
    else:
        expand, expand_spec = shape((2, ROWS, STEPS * HALF), BF), pl.BlockSpec((2, ROWS, HALF), lambda j: (0, 0, j))
    return pl.pallas_call(
        functools.partial(tail_back_kernel, layer),
        grid=(STEPS + 1 if layer == 0 else STEPS,),
        out_shape=(
            shape(WHOLE, BF), expand, shape((D, HALF), BF), shape((ROWS, D), F32), shape((ROWS, D), BF),
            shape((8, D), F32), shape((1, FF), F32),
        )
        + ((landing(0),) * 2 if carry else ()),
        in_specs=[
            full, full, full, pair if layer == 0 else ANY, pl.BlockSpec((2, ROWS, CHUNK), lambda j: (0, 0, at(j))),
            pl.BlockSpec((ROWS, CHUNK), lambda j: (0, at(j))), pair, square, wide, tall, vec, vec,
        ]
        + [ANY] * len(carry),
        out_specs=(
            chunk, expand_spec, pl.BlockSpec((D, HALF), lambda j: (0, 0)), full, full,
            pl.BlockSpec((8, D), lambda j: (0, 0)), pl.BlockSpec((1, CHUNK), lambda j: (0, at(j))),
        )
        + ((ANY,) * 2 if carry else ()),
        scratch_shapes=[
            pltpu.VMEM((ROWS, D), BF), pltpu.VMEM((ROWS, D), BF), pltpu.VMEM((STEPS, ROWS, CHUNK), BF), pltpu.VMEM((ROWS, D), F32),
            pltpu.VMEM((2, ROWS, HALF), BF), pltpu.VMEM((2, ROWS, HALF), BF), pltpu.VMEM((STEPS, 2, ROWS, HALF), BF),
            dma((STEPS + 2,)), dma((STEPS + 2,)),
        ]
        + ([dma((2, 3, 3)), dma((2, 3, 3))] if carry else []),
        compiler_params=pltpu.CompilerParams(collective_id=7 + layer, has_side_effects=True, vmem_limit_bytes=60 * MIB),
        name=f"tail_back_{layer}",
    )(g, saved["r1"], saved["r2"], saved["low_all"], saved["act_all"], saved["slope"], saved["mixed_all"],
      w["output_weight"], w["expand_weight"], w["reduce_weight"], w["first_gain"], w["second_gain"], *carry)


VECTORS = 24


def last_kernel(*refs):
    refs = list(refs)

    def take(count):
        out, refs[:count] = refs[:count], []
        return out

    rows, gq, parts, gres, dwo, wq, wk, wv = take(8)
    e0, got_e0, r0, got_r0, q0_two, got_q0_two, e0_two, got_e0_two, r1_two, got_r1_two = take(10)
    vec_p, vec, vec_e, vec_p_two, vec_two, vec_e_two = take(6)
    gh, fix_got, rfix_got, v_out = take(4)
    scratch = take(18)
    p0, got_q0, own_q0, s_q0, got_q1, s_q1, got_q2 = take(7)
    own_e0, held_e0, s_e0, got_e1, s_e1, got_e2 = take(6)
    own_r0, held_r0, s_r0, got_r1, s_r1, got_r2 = take(6)
    own_q0_two, held_q0_two, s_q0_two, got_q1_two, s_q1_two, got_q2_two = take(6)
    own_e0_two, held_e0_two, s_e0_two, got_e1_two, s_e1_two, got_e2_two = take(6)
    own_r1_two, held_r1_two, s_r1_two, got_r2_two = take(4)
    fix_send, rfix_send, vsum, vgot, vtotal, vz, vx = take(7)
    local, send, recv, fsend, frecv, vsend, vrecv = take(7)

    place = chip_place()
    core = lax.axis_index("blk_1")
    pos = lax.axis_index("dp_2") * 4 + lax.axis_index("blk_0") * 2 + core
    other = 1 - core
    sibling = {"blk_1": other}
    loads, flights = [], {}

    def start_loads():
        loads.extend(
            [
                begin(own_loads("e", 0, e0, own_e0, got_e0, held_e0, local.at[0])),
                begin(own_loads("r", 0, r0, own_r0, got_r0, held_r0, local.at[1])),
                begin(own_loads("q", 0, q0_two, own_q0_two, got_q0_two, held_q0_two, local.at[2])),
                begin(own_loads("e", 0, e0_two, own_e0_two, got_e0_two, held_e0_two, local.at[3])),
                begin(own_loads("r", 1, r1_two, own_r1_two, got_r1_two, held_r1_two, local.at[4])),
            ]
        )
        vectors = [vec_p[0:1], vec_p[1:2]] + [vec[k : k + 1] for k in range(6)]
        vectors += [vec_p_two[0:1], vec_p_two[1:2]] + [vec_two[k : k + 1] for k in range(6)]
        vectors += [v[:, k * D : (k + 1) * D] for v in (vec_e, vec_e_two) for k in range(4)]
        for k, vector in enumerate(vectors):
            vsum[k // 3, k % 3 : k % 3 + 1] = vector
        for k in range(8):
            vsum[k, 3:8] = jnp.zeros((5, D), F32)

    def launch(key, group, stage, source, got, n):
        flights[key] = begin(stage_copies(group, stage, source, got, send.at[n], recv.at[n]))

    def to_all(source, dest, at):
        out = []
        for d in range(1, 8):
            t = lax.rem(pos + d, 8)
            out.append(remote(source(t), dest.at[pos], vsend.at[at + d], vrecv.at[at + d], pos_device(t)))
        return begin(out)

    def along(axis, got, at):
        return begin([remote(vtotal, got.at[d - 1], vsend.at[at + d], vrecv.at[at + d], peer_of(axis, place, d)) for d in (1, 2, 3)])

    def greeted():
        flights["vc"] = to_all(lambda t: vsum.at[t], vgot, 0)
        end(loads[0])
        add_held(own_e0, held_e0, s_e0)
        launch("e1", "e", 1, s_e0, got_e1, 0)
        end(loads[1])
        add_held(own_r0, held_r0, s_r0)
        launch("r1", "r", 1, s_r0, got_r1, 1)
        end(loads[2])
        add_held(own_q0_two, held_q0_two, s_q0_two)
        launch("q1_two", "q", 1, s_q0_two, got_q1_two, 2)
        end(loads[3])
        add_held(own_e0_two, held_e0_two, s_e0_two)
        launch("e1_two", "e", 1, s_e0_two, got_e1_two, 3)
        end(loads[4])
        add_held(own_r1_two, held_r1_two, s_r1_two)
        launch("r2_two", "r", 2, s_r1_two, got_r2_two, 4)

    def far_done():
        end(flights["vc"])
        vgot[pos] = vsum[pos]
        total = vgot[0]
        for k in range(1, 8):
            total = total + vgot[k]
        vtotal[...] = total
        flights["vz"] = along(0, vz, 7)

    def square_flights(half):
        out = []
        for d in (2, 1, 3):
            for n, axis in ((1, 1), (2, 0)):
                at, two = lax.rem(place[axis] + d, 4), pl.ds(2 * half, 2)
                src = p0.at[1, two, :, at] if n == 1 else p0.at[2, two, at]
                sems = send.at[12 + half, n, d - 1], recv.at[12 + half, n, d - 1]
                out.append(remote(src, got_q0.at[n, d - 1, two], *sems, peer_of(axis, place, d)))
        return out

    def square_along_y(d):
        to = lax.rem(place[2] + d, 4)
        return remote(p0.at[0, to], got_q0.at[0, d - 1], send.at[5, 0, d - 1], recv.at[5, 0, d - 1], peer_of(2, place, d))

    def launch_squares(half):
        for d in (2, 1, 3):
            pl.when(lax.rem(place[2] + d, 4) // 2 == half)(lambda d=d: square_along_y(d).start())
        begin(square_flights(half))

    def two_squares():
        launch_squares(0)

    def squares():
        launch_squares(1)
        end(flights["vz"])
        vtotal[...] = vtotal[...] + vz[0] + vz[1] + vz[2]
        flights["vx"] = along(1, vx, 10)
        end(flights["e1"])
        add_direct("e", 1, s_e0, got_e1, s_e1)
        launch("e2", "e", 2, s_e1, got_e2, 7)
        end(flights["r1"])
        add_direct("r", 1, s_r0, got_r1, s_r1)
        launch("r2", "r", 2, s_r1, got_r2, 8)
        end(flights["q1_two"])
        add_direct("q", 1, s_q0_two, got_q1_two, s_q1_two)
        launch("q2_two", "q", 2, s_q1_two, got_q2_two, 6)
        end(flights["e1_two"])
        add_direct("e", 1, s_e0_two, got_e1_two, s_e1_two)
        launch("e2_two", "e", 2, s_e1_two, got_e2_two, 11)

    peers = axis_peers((0, 1)) + [pos_device(lax.rem(pos + d, 8)) for d in range(1, 8)]
    hooks = dict(loads=start_loads, greeted=greeted, far=far_done, two_squares=two_squares, squares=squares)
    project_back_body(0, rows, gq, parts, gres, dwo, wq, wk, wv, p0, gh, scratch, peers, hooks)

    def last(group, source, got):
        thirds = []
        for n in range(3):
            total = own_share(group, 2, n, source)[...].astype(F32)
            for d in range(3):
                total += got[n, d].astype(F32)
            thirds.append(total)
        return jnp.concatenate(thirds, axis=1)

    def rows_out(layer, part, total):
        for k in range(8):
            fix_send[layer, part, k, 0:6] = total[6 * k : 6 * k + 6]
        out = []
        for d in range(1, 8):
            t = lax.rem(pos + d, 8)
            sems = fsend.at[layer, part, d], frecv.at[layer, part, d]
            out.append(remote(fix_send.at[layer, part, t], fix_got.at[layer, part, pos], *sems, pos_device(t)))
        return begin(out)

    def reduce_out(layer, total):
        rfix_send[layer] = total
        there, here = [pl.ds(pl.multiple_of(c * 24, 8), 24) for c in (other, core)]
        rfix_got[layer, core] = rfix_send[layer, here]
        sems = fsend.at[layer, 0, 0], frecv.at[layer, 0, 0]
        return begin([remote(rfix_send.at[layer, there], rfix_got.at[layer, core], *sems, sibling)])

    end(flights["vx"])
    vtotal[...] = vtotal[...] + vx[0] + vx[1] + vx[2]
    fixes = to_all(lambda t: vtotal, v_out, 13)
    v_out[pos] = vtotal[...]
    end(flights["r2_two"])
    fixes += reduce_out(1, last("r", s_r1_two, got_r2_two))
    end(flights["e2"])
    fixes += rows_out(0, 1, last("e", s_e1, got_e2))
    end(flights["r2"])
    fixes += reduce_out(0, last("r", s_r1, got_r2))
    end(flights["q2_two"])
    fixes += rows_out(1, 0, last("q", s_q1_two, got_q2_two))
    end(flights["e2_two"])
    fixes += rows_out(1, 1, last("e", s_e1_two, got_e2_two))
    for n in range(3):
        own_q0[n] = own_share("q", 0, n, p0)[...]
    end([square_along_y(d) for d in (1, 2, 3)] + square_flights(0) + square_flights(1))
    add_held(own_q0, got_q0, s_q0)
    launch("q1", "q", 1, s_q0, got_q1, 9)
    end(flights["q1"])
    add_direct("q", 1, s_q0, got_q1, s_q1)
    launch("q2", "q", 2, s_q1, got_q2, 10)
    end(flights["q2"])
    fixes += rows_out(0, 0, last("q", s_q1, got_q2))
    for layer in range(2):
        for part in range(2):
            fix_got[layer, part, pos] = fix_send[layer, part, pos]
    end(fixes)


def last_step(rows_all, gq, parts, gres, dwo, w, carry, vecs):
    dma, shape = pltpu.SemaphoreType.DMA, jax.ShapeDtypeStruct
    own, got = own_scratch, got_scratch
    return pl.pallas_call(
        last_kernel,
        out_shape=(shape((ROWS, D), BF), shape((2, 2, 8, 8, HALF), F32), shape((2, 2, 24, HALF), F32), shape((8, 8, D), F32)),
        in_specs=[ANY] * 18 + [VMEM] * 6,
        out_specs=[VMEM] * 4,
        scratch_shapes=project_back_scratch(0)
        + [pltpu.VMEM(WHOLE, BF), got(0), own(0), own(0), got(1), own(1), got(2)]
        + [own(0), got(0), own(0), got(1), own(1), got(2)] * 4
        + [own(1), got(1), own(1), got(2)]
        + [
            pltpu.VMEM((2, 2, 8, 8, HALF), F32),
            pltpu.VMEM((2, 48, HALF), F32),
            pltpu.VMEM((8, 8, D), F32),
            pltpu.VMEM((8, 8, D), F32),
            pltpu.VMEM((8, D), F32),
            pltpu.VMEM((3, 8, D), F32),
            pltpu.VMEM((3, 8, D), F32),
            dma((5, 4)), dma((14, 3, 3)), dma((14, 3, 3)), dma((2, 2, 8)), dma((2, 2, 8)), dma((21,)), dma((21,)),
        ],
        compiler_params=pltpu.CompilerParams(collective_id=3, has_side_effects=True, vmem_limit_bytes=60 * MIB),
        name="last_step",
    )(rows_all, gq, parts.reshape(2, SLOTS * BLOCK, D), gres, dwo, w["query_weight"], w["key_weight"], w["value_weight"], *carry, *vecs)


def layer_forward(layer, h, table, w, out_type):
    q, kv_all, rows_all = project(layer, h, w)
    mixed = attend(layer, table, q, kv_all)
    r1, r2, out, slope, act_all, low_all, mixed_all = tail(layer, mixed, h, w, out_type)
    return out, dict(
        rows_all=rows_all, q=q, kv_all=kv_all, r1=r1, r2=r2, slope=slope, act_all=act_all, low_all=low_all, mixed_all=mixed_all
    )


def finish_kernel(quads, rows, vecs, final, grad, *outs):
    me = lax.axis_index(DP_BLK)
    wq, wk, wv, wo, we, wr, q_b, v_b, s_g, s_s, r_b, f_g, f_s, o_b, e_b, final_out, grad_out = outs
    final_out[...] = final[...]
    grad_out[...] = grad[...]
    for layer in range(2):
        for s in range(8):
            y, c = (s // 2 % 2) * 2 + s // 4, s % 2
            (wq, wo, wk, wv)[y][:, layer, c * HALF : (c + 1) * HALF] = quads[layer, 0, s, 0:6]
            we[:, layer, y * D + c * HALF : y * D + (c + 1) * HALF] = quads[layer, 1, s, 0:6]
        for c in range(2):
            wr[layer, :, c * HALF : (c + 1) * HALF] = rows[layer, c]
    vectors = [vecs[k // 3, k % 3 : k % 3 + 1] for k in range(VECTORS)]
    turned = pltpu.roll(jnp.concatenate(vectors[0:16], axis=0), lax.rem(D - 6 * me, D), 1)
    for n, out in enumerate((q_b, v_b, s_g, s_s, r_b, f_g, f_s, o_b)):
        for layer in range(2):
            out[layer : layer + 1] = turned[8 * layer + n : 8 * layer + n + 1, 0:6]
    wide = pltpu.roll(jnp.concatenate(vectors[16:24], axis=0), lax.rem(D - 24 * lax.rem(me, 32), D), 1)
    for layer in range(2):
        total = jnp.zeros((1, 24), F32)
        for k in range(4):
            total = total + jnp.where(me // 32 == k, wide[4 * layer + k : 4 * layer + k + 1, 0:24], 0.0)
        e_b[layer : layer + 1] = total


def finish(quads, rows, vecs, final, grad):
    shape = jax.ShapeDtypeStruct
    square, small, hidden = shape((6, 2, D), F32), shape((2, 6), F32), shape((1, ROWS, D), BF)
    outs = pl.pallas_call(
        finish_kernel,
        out_shape=(square,) * 4 + (shape((6, 2, FF), F32), shape((2, 24, D), F32)) + (small,) * 8 + (shape((2, 24), F32),)
        + (hidden, hidden),
        in_specs=[VMEM] * 5,
        out_specs=(VMEM,) * 17,
        name="finish",
    )(quads, rows, vecs, final[None], grad[None])
    wq, wk, wv, wo, we = [o.transpose(1, 0, 2) for o in outs[:5]]
    wr, q_b, v_b, s_g, s_s, r_b, f_g, f_s, o_b, e_b, final, grad = outs[5:]
    return (final, grad, wq, wk, wv, wo, q_b, v_b, o_b, we, e_b, wr, r_b, f_g, f_s, s_g, s_s)


NAMES = (
    "query_weight", "key_weight", "value_weight", "output_weight", "query_bias", "value_bias", "output_bias", "expand_weight",
    "expand_bias", "reduce_weight", "reduce_bias", "first_gain", "first_shift", "second_gain", "second_shift",
)


def local(hidden, output_grad, block_counts, slot_table, block_order_two, block_order_three, *weights):
    w = dict(zip(NAMES, weights))
    table = (slot_table, block_counts, block_order_two, block_order_three)
    middle, saved_one = layer_forward(0, hidden[0], table, w, F32)
    final, saved_two = layer_forward(1, middle, table, w, BF)
    r_two, gi, dwo, gres, gm, vec_two, vec_e_two = tail_back(1, output_grad[0], saved_two, w)
    gq, parts, vec_p_two, gi_other, got_r = attend_back(1, table, saved_two["q"], saved_two["kv_all"], gm, gi, r_two)
    carry = (gi, gi_other, r_two, got_r)
    q_two, grad_middle, e_two, r1, got_r = project_back_two(
        saved_two["rows_all"], gq, parts, gres, dwo, w, saved_two["low_all"], carry
    )
    r0, e0, dwo, gres, gm, vec, vec_e, got_q, got_e = tail_back(0, grad_middle, saved_one, w, (q_two, e_two))
    gq, parts, vec_p, got_e0, got_r0 = attend_back(0, table, saved_one["q"], saved_one["kv_all"], gm, e0, r0)
    carry = (e0, got_e0, r0, got_r0, q_two, got_q, e_two, got_e, r1, got_r)
    vecs = (vec_p, vec, vec_e, vec_p_two, vec_two, vec_e_two)
    grad_hidden, *sums = last_step(saved_one["rows_all"], gq, parts, gres, dwo, w, carry, vecs)
    return finish(*sums, final, grad_hidden)


def solution(mesh):
    finer = Mesh(mesh.devices.reshape(4, 4, 2, 2, 2), DP_BLK)
    in_specs = (P(DP, BLK, None), P(DP, BLK, None), P(DP), P(DP, None)) + (P(),) * 17
    wide, flat = P(None, DP_BLK, None), P(None, DP_BLK)
    out_specs = (P(DP, BLK, None), P(DP, BLK, None), wide, wide, wide, wide, flat, flat, flat, wide, flat, wide) + (flat,) * 5
    return jax.shard_map(local, mesh=finer, in_specs=in_specs, out_specs=out_specs, check_vma=False)
```

profile of v0, /device:TPU:1, one launch (start us, length us, event | category | flops | bytes accessed | tf_op | source)
XLA Modules:
  0.0 266.3 jit_solution(7061054917128836102)
XLA Ops:
  1.3 1.4 copy.44.two
  2.7 1.4 copy.45.three
  4.0 13.7 %project_0.1 = (bf16[384,768]{1,0:T(8,128)(2,1)}, bf16[2,1536,768]{2,1,0:T(8,128)(2,1)}, bf16[2,640,768]{2,1,0:T(8,128)(2,1)}) custom-call(bf16[384,768]{1,0:T(8,128)(2,1)} %bitcast.23, bf16[2,768,768]{2,1,0:T(8,128)(2,1)} %refs_5_.1, bf16[2,768,768]{2,1,0:T(8,128)(2,1)} %refs_6_.1, bf16[2,768,768]{2,1,0:T(8,128)(2,1)} %refs_7_.1, bf16[2,768]{1,0:T(2,128)(2,1)} %bq.3, ...), custom_call_target="tpu_custom_call" | custom-call | tf_op jit(solution)/shard_map/project_0/pallas_call | solution.py:294
  17.7 10.8 %attend_0.1.mixed = bf16[384,768]{1,0:T(8,128)(2,1)} custom-call(s32[1,3]{1,0:T(1,128)} %tab.7, s32[1]{0:T(128)S(6)} %copy.46.cnt, s32[12,2]{1,0:T(8,128)} %copy.44.two, s32[12,3]{1,0:T(8,128)} %copy.45.three, bf16[384,768]{1,0:T(8,128)(2,1)} %get-tuple-element.90.q, bf16[2,3,512,768]{3,2,1,0:T(8,128)(2,1)} %bitcast.13, bf16[2,3,512,768]{3,2,1,0:T(8,128)(2,1)} %bitcast.14), custom_call_target="tpu_custom_call" | custom-call | tf_op jit(solution)/shard_map/attend_0/pallas_call | solution.py:542
  28.5 14.1 %tail_0.1 = (f32[384,768]{1,0:T(8,128)}, f32[384,768]{1,0:T(8,128)}, f32[384,768]{1,0:T(8,128)}, bf16[384,3072]{1,0:T(8,128)(2,1)}, bf16[2,384,3072]{2,1,0:T(8,1...) custom-call(bf16[384,768]{1,0:T(8,128)(2,1)} %attend_0.1.mixed, bf16[384,768]{1,0:T(8,128)(2,1)} %bitcast.24, ...), custom_call_target="tpu_custom_call" | custom-call | tf_op jit(solution)/shard_map/tail_0/pallas_call | solution.py:708
  42.6 23.6 %project_1.1 = (bf16[384,768]{1,0:T(8,128)(2,1)}, bf16[2,1536,768]{2,1,0:T(8,128)(2,1)}, bf16[2,768,768]{2,1,0:T(8,128)(2,1)}) custom-call(f32[384,768]{1,0:T(8,128)} %get-tuple-element.92.h, bf16[2,768,768]{2,1,0:T(8,128)(2,1)} %refs_5_.1, bf16[2,768,768]{2,1,0:T(8,128)(2,1)} %refs_6_.1, bf16[2,768,768]{2,1,0:T(8,128)(2,1)} %refs_7_.1, bf16[2,768]{1,0:T(2,128)(2,1)} %bq.3, ...), custom_call_target="tpu_custom_call" | custom-call | tf_op jit(solution)/shard_map/project_1/pallas_call | solution.py:294
  66.2 11.1 %attend_1.1.mixed = bf16[384,768]{1,0:T(8,128)(2,1)} custom-call(s32[1,3]{1,0:T(1,128)} %tab.7, s32[1]{0:T(128)S(6)} %copy.46.cnt, s32[12,2]{1,0:T(8,128)} %copy.44.two, s32[12,3]{1,0:T(8,128)} %copy.45.three, bf16[384,768]{1,0:T(8,128)(2,1)} %get-tuple-element.94.q, bf16[2,3,512,768]{3,2,1,0:T(8,128)(2,1)} %bitcast.17, bf16[2,3,512,768]{3,2,1,0:T(8,128)(2,1)} %bitcast.18), custom_call_target="tpu_custom_call" | custom-call | tf_op jit(solution)/shard_map/attend_1/pallas_call | solution.py:542
  77.3 14.0 %tail_1.1 = (f32[384,768]{1,0:T(8,128)}, f32[384,768]{1,0:T(8,128)}, bf16[384,768]{1,0:T(8,128)(2,1)}, bf16[384,3072]{1,0:T(8,128)(2,1)}, bf16[2,384,3072]{2,1,0...) custom-call(bf16[384,768]{1,0:T(8,128)(2,1)} %attend_1.1.mixed, ...), custom_call_target="tpu_custom_call" | custom-call | tf_op jit(solution)/shard_map/tail_1/pallas_call | solution.py:708
  91.3 19.3 %tail_back_1.1 = (bf16[3,4,4,4,48,128]{5,4,3,2,1,0:T(8,128)(2,1)}, bf16[2,384,1536]{2,1,0:T(8,128)(2,1)}, bf16[768,384]{1,0:T(8,128)(2,1)}, f32[384,768]{1,0:T(8...) custom-call(bf16[384,768]{1,0:T(8,128)(2,1)} %bitcast.27, f32[384,768]{1,0:T(8,128)} %get-tuple-element.96.r1, ...), custom_call_target="tpu_custom_call" | custom-call | tf_op jit(solution)/shard_map/tail_back_1/pallas_call | solution.py:845
  110.7 19.3 %attend_back_1.1 = (bf16[384,768]{1,0:T(8,128)(2,1)}, bf16[2,3,512,768]{3,2,1,0:T(8,128)(2,1)}, f32[2,768]{1,0:T(2,128)}, bf16[384,1536]{1,0:T(8,128)(2,1)}, bf16[3,3,4,4,48,128]{5,4,3,2,1,0:T(8,128)(2,1)}) custom-call(s32[1,3]{1,0:T(1,128)} %tab.7, s32[1]{0:T(128)S(6)} %copy.46.cnt, s32[12,2]{1,0:T(8,128)} %copy.44.two, s32[12,3]{1,0:T(8,128)} %copy.45.three, ...), custom_call_target="tpu_custom_call" | custom-call | tf_op jit(solution)/shard_map/attend_back_1/pallas_call | solution.py:634
  130.0 28.3 %project_back_1.1 = (bf16[3,4,4,4,48,128]{5,4,3,2,1,0:T(8,128)(2,1)}, f32[384,768]{1,0:T(8,128)}, bf16[3,4,4,4,48,128]{5,4,3,2,1,0:T(8,128)(2,1)}, bf16[3,4,4,48...) custom-call(bf16[2,768,768]{2,1,0:T(8,128)(2,1)} %get-tuple-element.93.rows, bf16[384,768]{1,0:T(8,128)(2,1)} %get-tuple-element.105.gq, ...), custom_call_target="tpu_custom_call" | custom-call | tf_op jit(solution)/shard_map/project_back_1/pallas_call | solution.py:468
  158.3 28.5 %tail_back_0.1 = (bf16[3,4,4,4,48,128]{5,4,3,2,1,0:T(8,128)(2,1)}, bf16[3,4,4,4,48,128]{5,4,3,2,1,0:T(8,128)(2,1)}, bf16[768,384]{1,0:T(8,128)(2,1)}, f32[384,76...) custom-call(f32[384,768]{1,0:T(8,128)} %get-tuple-element.111.g, ...), custom_call_target="tpu_custom_call" | custom-call | tf_op jit(solution)/shard_map/tail_back_0/pallas_call | solution.py:845
  186.8 25.4 %attend_back_0.1 = (bf16[384,768]{1,0:T(8,128)(2,1)}, bf16[2,3,512,768]{3,2,1,0:T(8,128)(2,1)}, f32[2,768]{1,0:T(2,128)}, bf16[3,3,4,4,48,128]{5,4,3,2,1,0:T(8,128)(2,1)}, bf16[3,3,4,4,48,128]{5,4,3,2,1,0:T(8,128)(2,1)}) custom-call(s32[1,3]{1,0:T(1,128)} %tab.7, s32[1]{0:T(128)S(6)} %copy.46.cnt, s32[12,2]{1,0:T(8,128)} %copy.44.two, s32[12,3]{1,0:T(8,128)} %copy.45.three, ...), custom_call_target="tpu_custom_call" | custom-call | tf_op jit(solution)/shard_map/attend_back_0/pallas_call | solution.py:634
  212.2 51.1 %last_step.1 = (bf16[384,768]{1,0:T(8,128)(2,1)}, f32[2,2,8,8,384]{4,3,2,1,0:T(8,128)}, f32[2,2,24,384]{3,2,1,0:T(8,128)}, f32[8,8,768]{2,1,0:T(8,128)}) custom-call(bf16[2,640,768]{2,1,0:T(8,128)(2,1)} %get-tuple-element.89.refs_0_, bf16[384,768]{1,0:T(8,128)(2,1)} %get-tuple-element.123.refs_1_, bf16[2,1536,768]{2,1,0:T(8,128)(2,1)} %bitcast.21, ...), custom_call_target="tpu_custom_call" | custom-call | tf_op jit(solution)/shard_map/last_step/pallas_call | solution.py:1067
  263.3 2.8 %finish.1 = (f32[6,2,768]{2,1,0:T(2,128)}, f32[6,2,768]{2,1,0:T(2,128)}, f32[6,2,768]{2,1,0:T(2,128)}, f32[6,2,768]{2,1,0:T(2,128)}, f32[6,2,3072]{2,1,0:T(2,128...) custom-call(f32[2,2,8,8,384]{4,3,2,1,0:T(8,128)} %get-tuple-element., ...), custom_call_target="tpu_custom_call" | custom-call | tf_op jit(solution)/shard_map/finish/pallas_call | solution.py:1128
where the time goes:
time: 269 us; the launch traced here: 266 us
  Pallas kernels  262 us (97%)
  local copies, waits for them, and re-layouts  2.72 us (1%)
    pallas_call x1, Pallas kernels, last_step(): pl.pallas_call(last_kernel, out_shape=(shape((ROWS, D), BF), shape((2, 2,...  51.1 us
    pallas_call x2, Pallas kernels, tail_back(): pl.pallas_call(functools.partial(tail_back_kernel, layer), grid=(STEPS +...  47.8 us
    pallas_call x2, Pallas kernels, attend_back(): pl.pallas_call(functools.partial(attend_back_kernel, layer), grid=(HEADS...  44.7 us
    pallas_call x2, Pallas kernels, project(): pl.pallas_call(functools.partial(project_kernel, layer), out_shape=(shape...  37.3 us
    pallas_call x1, Pallas kernels, project_back_two(): pl.pallas_call(project_back_two_kernel, out_shape=(shape(WHOLE, BF), shap...  28.3 us
    pallas_call x2, Pallas kernels, tail(): pl.pallas_call(functools.partial(tail_kernel, layer), grid=(STEPS,), out_...  28.1 us
    pallas_call x2, Pallas kernels, attend(): pl.pallas_call(functools.partial(attend_kernel, layer), grid=(HEADS // 2,...  21.9 us

commit v1 on v0

--- a/solution.py
+++ b/solution.py
@@ -218,6 +218,7 @@
 
 
 FAR = (256, ROWS)
+EARLY = 192
 
 
 def far_plan(layer, y_hi, core, block):
@@ -229,82 +230,6 @@
 
 def is_middle(block):
     return jnp.logical_and(block >= 1, block <= 2)
-
-
-def project_kernel(
-    layer, h, wq, wk, wv, bq, bv, q, kv_all, rows_all, low, kv, far, kv_far, held_q, held_k, held_v, late, local, send, recv
-):
-    wk, wv = Late(wk.at[layer], held_k, late.at[0]), Late(wv.at[layer], held_v, late.at[1])
-    wq = Late(wq.at[layer], held_q, late.at[2])
-    y_hi, core, block = places()
-    far_rows = FAR[layer]
-    sibling = {"blk_1": 1 - core}
-    partner, give, theirs = far_plan(layer, y_hi, core, block)
-    low[...] = h[...].astype(BF)
-    greet([sibling, partner])
-    hidden = remote(low.at[rows_at(give, far_rows)], far, send.at[0], recv.at[0], partner)
-
-    def talk(step):
-        if layer == 0:
-            pl.when(is_middle(block))(step)
-        else:
-            step()
-
-    def both(src, dst, n):
-        return [remote(src, dst, send.at[n], recv.at[n], sibling), pltpu.make_async_copy(src, dst, local.at[n])]
-
-    talk(lambda: hidden.start())
-    copies = both(low, rows_all.at[core, pl.ds(0, ROWS)], 1)
-    kv[0] = dot(low[...], wk()[...]).astype(BF)
-    kv[1] = (dot(low[...], wv()[...]) + row_of(bv, layer)).astype(BF)
-    copies += both(kv, kv_all.at[:, rows_at(block * ROWS, ROWS)], 2)
-    for c in copies:
-        c.start()
-    q[...] = (dot(low[...], wq()[...]) + row_of(bq, layer)).astype(BF)
-    far_place = kv_all.at[:, rows_at(theirs, far_rows)]
-    keep_far = pltpu.make_async_copy(kv_far, far_place, local.at[3])
-
-    def far_keys():
-        kv_far[0] = dot(far[...], wk()[...]).astype(BF)
-        kv_far[1] = (dot(far[...], wv()[...]) + row_of(bv, layer)).astype(BF)
-        keep_far.start()
-
-    talk(lambda: hidden.wait())
-    if layer == 0:
-
-        @pl.when(jnp.logical_not(is_middle(block)))
-        def _():
-            far[...] = jnp.zeros_like(far)
-
-    last = both(far, rows_all.at[core, pl.ds(ROWS, far_rows)], 4)
-    for c in last:
-        c.start()
-    talk(far_keys)
-    if layer == 1:
-        relay = remote(kv_far, far_place, send.at[3], recv.at[3], sibling)
-        relay.start()
-        relay.wait()
-    talk(lambda: keep_far.wait())
-    for c in copies + last:
-        c.wait()
-
-
-def project(layer, h, w):
-    shape, dma, far_rows = jax.ShapeDtypeStruct, pltpu.SemaphoreType.DMA, FAR[layer]
-    q, kv_all, rows_all = pl.pallas_call(
-        functools.partial(project_kernel, layer),
-        out_shape=(shape((ROWS, D), BF), shape((2, SLOTS * BLOCK, D), BF), shape((2, ROWS + far_rows, D), BF)),
-        in_specs=[VMEM, ANY, ANY, ANY, VMEM, VMEM],
-        out_specs=(VMEM, ANY, ANY),
-        scratch_shapes=[
-            pltpu.VMEM((ROWS, D), BF), pltpu.VMEM((2, ROWS, D), BF), pltpu.VMEM((far_rows, D), BF),
-            pltpu.VMEM((2, far_rows, D), BF), pltpu.VMEM((D, D), BF), pltpu.VMEM((D, D), BF), pltpu.VMEM((D, D), BF), dma((3,)),
-            dma((5,)), dma((5,)), dma((5,)),
-        ],
-        compiler_params=pltpu.CompilerParams(collective_id=1 + layer, has_side_effects=True, vmem_limit_bytes=60 * MIB),
-        name=f"project_{layer}",
-    )(h, w["query_weight"], w["key_weight"], w["value_weight"], w["query_bias"], w["value_bias"])
-    return q, kv_all.reshape(2, SLOTS, BLOCK, D), rows_all
 
 
 def project_back_body(layer, rows, gq, parts, gres, dwo, wq, wk, wv, p0, gh, scratch, peers, hooks):
@@ -504,30 +429,14 @@
     return jnp.where(left_lanes(PIECE), both[:PIECE], both[PIECE:])
 
 
+def own_rows(both):
+    top = lax.broadcasted_iota(jnp.int32, (2 * HD, PIECE), 0) < HD
+    return jnp.where(top, both[:, :PIECE], both[:, PIECE:]).T
+
+
 def slot_mask(s0, s1, t, kind):
     first, second = jnp.where(s0 == t, 1.0, 0.0), jnp.where(s1 == t, 1.0, 0.0)
     return jnp.where(left_lanes(), first, second).astype(kind)
-
-
-def soft(scores):
-    top = jnp.max(scores, axis=0, keepdims=True)
-    e = jnp.exp((scores - top) * SCALE)
-    return e * (1.0 / jnp.sum(e, axis=0, keepdims=True))
-
-
-def attend_kernel(layer, tab, cnt, two, three, q, k, v, mixed):
-    pair = pl.program_id(0)
-    left = left_lanes(BLOCK)
-    for i in range(3):
-        rows = pl.ds(i * PIECE, PIECE)
-        s0, live = slots_of(layer, tab, cnt, two, three, i, 2 * pair)
-        if layer == 0:
-            keys, values = k[s0], v[s0]
-        else:
-            s1, _ = slots_of(layer, tab, cnt, two, three, i, 2 * pair + 1)
-            keys, values = jnp.where(left, k[s0], k[s1]), jnp.where(left, v[s0], v[s1])
-        weights = soft(dot_nt(keys, two_heads(q[rows, :]))).astype(BF)
-        mixed[rows, :] = (own_columns(dot_tn(weights, values)) * live).astype(BF)
 
 
 def attend_specs():
@@ -535,19 +444,6 @@
     keys = pl.BlockSpec((None, SLOTS, BLOCK, 2 * HD), lambda p: (0, 0, 0, p))
     values = pl.BlockSpec((None, SLOTS, BLOCK, 2 * HD), lambda p: (1, 0, 0, p))
     return tile, keys, values
-
-
-def attend(layer, table, q, kv_all):
-    tile, keys, values = attend_specs()
-    return pl.pallas_call(
-        functools.partial(attend_kernel, layer),
-        grid=(HEADS // 2,),
-        out_shape=jax.ShapeDtypeStruct((ROWS, D), BF),
-        in_specs=[SMEM] * 4 + [tile, keys, values],
-        out_specs=tile,
-        compiler_params=params(),
-        name=f"attend_{layer}",
-    )(*table, q, kv_all, kv_all)
 
 
 def attend_back_step(layer, tab, cnt, two, three, q, k, v, gm, gq, gkv, acc):
@@ -566,14 +462,17 @@
             masks.append([slot_mask(s0, s1, t, F32) for t in range(SLOTS)])
             keys = k[0] * low[0] + k[1] * low[1] + k[2] * low[2]
             values = v[0] * low[0] + v[1] * low[1] + v[2] * low[2]
-        qq = two_heads(q[rows, :])
+        qq = two_heads(q[rows, :] * jnp.asarray(SCALE, BF))
         gg = two_heads((gm[rows, :].astype(F32) * live).astype(BF))
-        weights = soft(dot_nt(keys, qq))
+        scores = dot_nt(keys, qq)
+        exps = jnp.exp(scores - jnp.max(scores, axis=0, keepdims=True))
+        factor = 1.0 / jnp.sum(exps, axis=0, keepdims=True)
         grad_weights = dot_nt(values, gg)
-        delta = jnp.sum(weights * grad_weights, axis=0, keepdims=True)
+        delta = jnp.sum(exps * grad_weights, axis=0, keepdims=True) * factor
+        weights = exps * factor
         grad_scores = (weights * (grad_weights - delta)).astype(BF)
-        gq[rows, :] = (own_columns(dot_tn(grad_scores, keys)) * SCALE).astype(BF)
-        gk = dot(grad_scores, qq) * SCALE
+        gq[rows, :] = (own_rows(dot_tn(keys, grad_scores)) * SCALE).astype(BF)
+        gk = dot(grad_scores, qq)
         gv = dot(weights.astype(BF), gg)
         if layer == 0:
             acc[0, s0] += gk
@@ -607,6 +506,9 @@
         barrier = pltpu.get_barrier_semaphore()
         for peer in peers:
             pl.semaphore_signal(barrier, inc=1, device_id=peer, device_id_type=MESH)
+        if layer == 0:
+            pl.semaphore_wait(barrier, len(peers))
+            begin(carried())
 
     attend_back_step(layer, tab, cnt, two, three, q, k, v, gm, gq, gkv, acc)
     vec[0:1] = jnp.sum(gq[...].astype(F32), axis=0, keepdims=True)
@@ -616,10 +518,12 @@
         total += live * jnp.sum(gm[i * PIECE : (i + 1) * PIECE, :].astype(F32), axis=0, keepdims=True)
     vec[1:2] = total
 
-    @pl.when(step == 0)
-    def _():
-        pl.semaphore_wait(pltpu.get_barrier_semaphore(), len(peers))
-        begin(carried())
+    if layer == 1:
+
+        @pl.when(step == 0)
+        def _():
+            pl.semaphore_wait(pltpu.get_barrier_semaphore(), len(peers))
+            begin(carried())
 
     @pl.when(step == HEADS // 2 - 1)
     def _():
@@ -646,228 +550,418 @@
 STEPS = FF // CHUNK
 
 
-def tail_kernel(
-    layer, mixed, h, wo, bo, g1, s1, we, be, wr, br, g2, s2, r1, r2, out, slope, act_all, low_all, mixed_all,
-    first, total, low, act, local, send, recv,
-):
-    j = pl.program_id(0)
-    core = lax.axis_index("blk_1")
+def chunk_columns(j):
+    return pl.ds(j * CHUNK, CHUNK)
+
+
+def project_part(layer, h, early, wq, wk, wv, bq, bv, q, kv_all, rows_all, low, far, local, send, recv):
+    y_hi, core, block = places()
+    far_rows = FAR[layer]
     sibling = {"blk_1": 1 - core}
-
-    def both(src, dst, n):
-        return [remote(src, dst, send.at[n], recv.at[n], sibling), pltpu.make_async_copy(src, dst, local.at[n])]
-
-    def act_copies(at):
-        return both(act.at[at], act_all.at[core, :, columns_at(at * CHUNK, CHUNK)], at)
-
-    early = both(mixed, mixed_all.at[core], STEPS) + both(low, low_all.at[core], STEPS + 1)
-
-    @pl.when(j == 0)
-    def _():
-        barrier = pltpu.get_barrier_semaphore()
-        pl.semaphore_signal(barrier, inc=1, device_id=sibling, device_id_type=MESH)
-        residual = h[...].astype(F32) + dot(mixed[...], wo[...]) + row_of(bo, layer)
-        r1[...] = residual
-        normed, _ = norm_parts(residual)
-        first[...] = normed * row_of(g1, layer) + row_of(s1, layer)
-        low[...] = first[...].astype(BF)
-        total[...] = jnp.zeros_like(total)
-        pl.semaphore_wait(barrier, 1)
-        for c in early:
-            c.start()
-
-    inner = dot(low[...], we[...]) + be[layer : layer + 1, columns_at(j * CHUNK, CHUNK)].astype(F32)
-    phi = 0.5 * (1.0 + lax.erf(inner * ROOT_HALF))
-    low_act = (inner * phi).astype(BF)
-    act[j] = low_act
-    for c in act_copies(j):
-        c.start()
-    slope[...] = (phi + inner * (INV_ROOT_TAU * jnp.exp(-0.5 * inner * inner))).astype(BF)
-    total[...] += dot(low_act, wr[...])
-
-    @pl.when(j == STEPS - 1)
-    def _():
-        residual = first[...] + total[...] + row_of(br, layer)
-        r2[...] = residual
-        normed, _ = norm_parts(residual)
-        out[...] = (normed * row_of(g2, layer) + row_of(s2, layer)).astype(out.dtype)
-        for c in early:
-            c.wait()
-        for at in range(STEPS):
-            for c in act_copies(at):
-                c.wait()
-
-
-def tail(layer, mixed, h, w, out_type):
-    square = layer_block(layer, (D, D), lambda j: (0, 0))
-    wide = layer_block(layer, (D, CHUNK), lambda j: (0, j))
-    tall = layer_block(layer, (CHUNK, D), lambda j: (j, 0))
-    full = pl.BlockSpec((ROWS, D), lambda j: (0, 0))
-    vec, dma = VMEM, pltpu.SemaphoreType.DMA
-    shape = jax.ShapeDtypeStruct
-    return pl.pallas_call(
-        functools.partial(tail_kernel, layer),
-        grid=(STEPS,),
-        out_shape=(
-            shape((ROWS, D), F32), shape((ROWS, D), F32), shape((ROWS, D), out_type), shape((ROWS, FF), BF),
-            shape((2, ROWS, FF), BF), shape((2, ROWS, D), BF), shape((2, ROWS, D), BF),
-        ),
-        in_specs=[full, full, square, vec, vec, vec, wide, vec, tall, vec, vec, vec],
-        out_specs=(full, full, full, pl.BlockSpec((ROWS, CHUNK), lambda j: (0, j)), ANY, ANY, ANY),
-        scratch_shapes=[
-            pltpu.VMEM((ROWS, D), F32), pltpu.VMEM((ROWS, D), F32), pltpu.VMEM((ROWS, D), BF),
-            pltpu.VMEM((STEPS, ROWS, CHUNK), BF), dma((STEPS + 2,)), dma((STEPS + 2,)), dma((STEPS + 2,)),
-        ],
-        compiler_params=pltpu.CompilerParams(collective_id=5 + layer, has_side_effects=True, vmem_limit_bytes=60 * MIB),
-        name=f"tail_{layer}",
-    )(mixed, h, w["output_weight"], w["output_bias"], w["first_gain"], w["first_shift"], w["expand_weight"], w["expand_bias"],
-      w["reduce_weight"], w["reduce_bias"], w["second_gain"], w["second_shift"])
-
-
-def tail_back_kernel(layer, g, r1, r2, low_all, act_all, slope, mixed_all, wo, we, wr, g1, g2, *refs):
+    partner, give, theirs = far_plan(layer, y_hi, core, block)
+    low[...] = h[...].astype(BF)
+    first = 0 if layer == 0 else EARLY
+    rest = far.at[pl.ds(first, far_rows - first)]
+    hidden = remote(low.at[pl.ds(pl.multiple_of(give + first, 64), far_rows - first)], rest, send.at[0], recv.at[0], partner)
+
+    def talk(step):
+        if layer == 0:
+            pl.when(is_middle(block))(step)
+        else:
+            step()
+
+    talk(lambda: hidden.start())
+    if layer == 1:
+        there = pltpu.make_async_copy(early, far.at[pl.ds(0, EARLY)], local.at[0])
+        there.start()
+    own_dst = rows_all.at[core, pl.ds(0, ROWS)]
+    copies = begin([remote(low, own_dst, send.at[1], recv.at[1], sibling), pltpu.make_async_copy(low, own_dst, local.at[1])])
+
+    def keys_of(source, count, start):
+        at = rows_at(start, count) if count % PIECE == 0 else pl.ds(pl.multiple_of(start, 64), count)
+        kv_all[0, at] = dot(source, wk()[...]).astype(BF)
+        kv_all[1, at] = (dot(source, wv()[...]) + row_of(bv, layer)).astype(BF)
+        return kv_all.at[:, at]
+
+    mine = keys_of(low[...], ROWS, block * ROWS)
+    copies += begin([remote(mine, mine, send.at[2], recv.at[2], sibling)])
+    q[...] = (dot(low[...], wq()[...]) + row_of(bq, layer)).astype(BF)
+    if layer == 1:
+        there.wait()
+        part = keys_of(far[0:EARLY], EARLY, theirs)
+        copies += begin([remote(part, part, send.at[3], recv.at[3], sibling)])
+    talk(lambda: hidden.wait())
+    if layer == 0:
+
+        @pl.when(jnp.logical_not(is_middle(block)))
+        def _():
+            far[...] = jnp.zeros_like(far)
+
+    far_dst = rows_all.at[core, pl.ds(ROWS, far_rows)]
+    copies += begin([remote(far, far_dst, send.at[4], recv.at[4], sibling), pltpu.make_async_copy(far, far_dst, local.at[2])])
+    if layer == 0:
+        talk(lambda: keys_of(far[...], far_rows, theirs) and None)
+    else:
+        part = keys_of(far[first:far_rows], far_rows - first, theirs + first)
+        copies += begin([remote(part, part, send.at[5], recv.at[5], sibling)])
+    end(copies)
+
+
+def attend_part(layer, table, q, kv_all, mixed):
+    @pl.loop(0, HEADS // 2)
+    def _(pair):
+        columns = columns_at(pair * 2 * HD, 2 * HD)
+
+        def tile(side, slot):
+            return kv_all[side, pl.ds(slot * BLOCK, BLOCK) if isinstance(slot, int) else rows_at(slot * BLOCK, BLOCK), columns]
+
+        for i in range(3):
+            rows = pl.ds(i * PIECE, PIECE)
+            s0, live = slots_of(layer, *table, i, 2 * pair)
+            if layer == 0:
+                keys, values = tile(0, s0), tile(1, s0)
+            else:
+                s1, _ = slots_of(layer, *table, i, 2 * pair + 1)
+                masks = [slot_mask(s0, s1, t, BF) for t in range(SLOTS)]
+                keys, values = [sum(tile(side, t) * masks[t] for t in range(SLOTS)) for side in (0, 1)]
+            scores = dot_nt(two_heads(q[rows, columns] * jnp.asarray(SCALE, BF)), keys)
+            exps = jnp.exp(scores - jnp.max(scores, axis=1, keepdims=True))
+            factor = live / jnp.sum(exps, axis=1, keepdims=True)
+            mixed[rows, columns] = own_columns(dot(exps.astype(BF), values) * factor).astype(BF)
+
+
+def tail_rows(layer, rows, h, mixed, wo, wes, wrs, vectors, r1, first, low, slope, r2, store, after_low):
+    bo, g1, s1, be, br, g2, s2 = vectors
+    residual = h[rows, :].astype(F32) + dot(mixed[rows, :], wo()[...]) + row_of(bo, layer)
+    r1[rows, :] = residual
+    normed, _ = norm_parts(residual)
+    first[rows, :] = normed * row_of(g1, layer) + row_of(s1, layer)
+    low[rows, :] = first[rows, :].astype(BF)
+    after_low()
+    total = first[rows, :] + row_of(br, layer)
+    for j in range(STEPS):
+        inner = dot(low[rows, :], wes[j]()[...]) + be[layer : layer + 1, j * CHUNK : (j + 1) * CHUNK].astype(F32)
+        phi = 0.5 * (1.0 + lax.erf(inner * ROOT_HALF))
+        low_act = (inner * phi).astype(BF)
+        slope[j, rows, :] = (phi + inner * (INV_ROOT_TAU * jnp.exp(-0.5 * inner * inner))).astype(BF)
+        store(j, low_act)
+        total = total + dot(low_act, wrs[j]()[...])
+    r2[rows, :] = total
+    normed, _ = norm_parts(total)
+    return normed * row_of(g2, layer) + row_of(s2, layer)
+
+
+def weight_loads(layer, wq, wk, wv, wo, we, wr, held, sems):
+    held_q, held_k, held_v, held_o, held_e, held_r = held
+    wk, wv = Late(wk.at[layer], held_k, sems.at[0]), Late(wv.at[layer], held_v, sems.at[1])
+    wq, wo = Late(wq.at[layer], held_q, sems.at[2]), Late(wo.at[layer], held_o, sems.at[3])
+    wes = [Late(we.at[layer, :, chunk_columns(j)], held_e.at[j], sems.at[4 + 2 * j]) for j in range(STEPS)]
+    wrs = [Late(wr.at[layer, chunk_columns(j)], held_r.at[j], sems.at[5 + 2 * j]) for j in range(STEPS)]
+    return wq, wk, wv, wo, wes, wrs
+
+
+def weight_scratch():
+    square = pltpu.VMEM((D, D), BF)
+    return [square] * 4 + [pltpu.VMEM((STEPS, D, CHUNK), BF), pltpu.VMEM((STEPS, CHUNK, D), BF), pltpu.SemaphoreType.DMA((2 * STEPS + 4,))]
+
+
+def project_scratch(layer):
+    dma = pltpu.SemaphoreType.DMA
+    return [
+        pltpu.VMEM((2, SLOTS * BLOCK, D), BF), pltpu.VMEM((ROWS, D), BF), pltpu.VMEM((FAR[layer], D), BF),
+        dma((3,)), dma((6,)), dma((6,)),
+    ]
+
+
+def first_layer_kernel(tab, cnt, two, three, h, wq, wk, wv, wo, we, wr, bq, bv, bo, g1, s1, be, br, g2, s2, *refs):
     refs = list(refs)
 
     def take(count):
         out, refs[:count] = refs[:count], []
         return out
 
-    q_in, e_in = take(2) if layer == 0 else (None, None)
-    dwr, dwe, dwo, gres, gm, vec, vec_e = take(7)
-    got_q, got_e = take(2) if layer == 0 else (None, None)
-    go, ga, gi, total, gocat, gacat, gicat, send, recv = take(9)
-    last = STEPS if layer == 0 else STEPS - 1
-
-    def carried():
-        if layer == 1:
-            return []
-        csend, crecv = refs
-        return stage_copies("q", 0, q_in, got_q, csend.at[0], crecv.at[0]) + stage_copies(
-            "e", 0, e_in, got_e, csend.at[1], crecv.at[1]
-        )
-
-    j = pl.program_id(0)
+    q, kv_out, rows_all, r1_out, r2, out, slope_out, act_all, low_all, mixed_all, ahead = take(11)
+    held, (wsems,) = take(6), take(1)
+    kv_all, low_in, far, plocal, psend, precv = take(6)
+    mixed, r1, first, low, act, slope, next_low, local, send, recv = take(10)
+    y_hi, core, _ = places()
+    sibling, partner = {"blk_1": 1 - core}, {"blk_0": 1 - y_hi}
+    wq, wk, wv, wo, wes, wrs = weight_loads(0, wq, wk, wv, wo, we, wr, held, wsems)
+    greet([sibling, partner, {"blk_0": 1 - y_hi, "blk_1": 1 - core}])
+    project_part(0, h, None, wq, wk, wv, bq, bv, q, kv_all, rows_all, low_in, far, plocal, psend, precv)
+    copies = begin([pltpu.make_async_copy(kv_all, kv_out, local.at[2 * STEPS + 3])])
+    attend_part(0, (tab, cnt, two, three), q, kv_all, mixed)
+
+    def both(src, dst, n):
+        return [remote(src, dst, send.at[n], recv.at[n], sibling), pltpu.make_async_copy(src, dst, local.at[n])]
+
+    copies += begin(both(mixed, mixed_all.at[core], STEPS))
+    parts = [(0, EARLY), (EARLY, ROWS - EARLY)]
+    for n, (start, count) in enumerate(parts):
+        rows = pl.ds(start, count)
+        final = n == len(parts) - 1
+
+        def after_low():
+            if final:
+                copies.extend(begin(both(low, low_all.at[core], STEPS + 1)))
+                copies.extend(begin([pltpu.make_async_copy(r1, r1_out, local.at[STEPS + 2])]))
+
+        def store(j, low_act):
+            act[j, rows, :] = low_act
+            if final:
+                copies.extend(begin(both(act.at[j], act_all.at[core, j], j)))
+                copies.extend(
+                    begin([pltpu.make_async_copy(slope.at[j], slope_out.at[:, chunk_columns(j)], local.at[STEPS + 3 + j])])
+                )
+
+        vectors = (bo, g1, s1, be, br, g2, s2)
+        result = tail_rows(0, rows, h, mixed, wo, wes, wrs, vectors, r1, first, low, slope, r2, store, after_low)
+        out[rows, :] = result
+        if n == 0:
+            next_low[...] = result.astype(BF)
+            copies.extend(begin([remote(next_low, ahead, send.at[STEPS + 2], recv.at[STEPS + 2], partner)]))
+    end(copies)
+
+
+def weight_args(w):
+    names = ("query_weight", "key_weight", "value_weight", "output_weight", "expand_weight", "reduce_weight", "query_bias",
+             "value_bias", "output_bias", "first_gain", "first_shift", "expand_bias", "reduce_bias", "second_gain", "second_shift")
+    return [w[name] for name in names]
+
+
+def first_layer(h, table, w):
+    dma, shape = pltpu.SemaphoreType.DMA, jax.ShapeDtypeStruct
+    low, full = shape((ROWS, D), BF), shape((ROWS, D), F32)
+    pair = shape((2, ROWS, D), BF)
+    q, kv_all, rows_all, r1, r2, out, slope, act_all, low_all, mixed_all, early = pl.pallas_call(
+        first_layer_kernel,
+        out_shape=(
+            low, shape((2, SLOTS * BLOCK, D), BF), shape((2, ROWS + FAR[0], D), BF), full, full, full, shape((ROWS, FF), BF),
+            shape((2, STEPS, ROWS, CHUNK), BF), pair, pair, shape((EARLY, D), BF),
+        ),
+        in_specs=[SMEM] * 4 + [VMEM] + [ANY] * 6 + [VMEM] * 9,
+        out_specs=(VMEM, ANY, ANY, ANY, VMEM, VMEM, ANY, ANY, ANY, ANY, ANY),
+        scratch_shapes=weight_scratch() + project_scratch(0)
+        + [pltpu.VMEM((ROWS, D), BF), pltpu.VMEM((ROWS, D), F32), pltpu.VMEM((ROWS, D), F32), pltpu.VMEM((ROWS, D), BF)]
+        + [pltpu.VMEM((STEPS, ROWS, CHUNK), BF)] * 2
+        + [pltpu.VMEM((EARLY, D), BF), dma((2 * STEPS + 4,)), dma((STEPS + 3,)), dma((STEPS + 3,))],
+        compiler_params=pltpu.CompilerParams(collective_id=1, has_side_effects=True, vmem_limit_bytes=60 * MIB),
+        name="first_layer",
+    )(*table, h, *weight_args(w))
+    saved = dict(
+        rows_all=rows_all, q=q, kv_all=kv_all.reshape(2, SLOTS, BLOCK, D), r1=r1, r2=r2, slope=slope, act_all=act_all,
+        low_all=low_all, mixed_all=mixed_all,
+    )
+    return out, early, saved
+
+
+def second_layer_kernel(tab, cnt, two, three, h, early, g, wq, wk, wv, wo, we, wr, bq, bv, bo, g1, s1, be, br, g2, s2, *refs):
+    refs = list(refs)
+
+    def take(count):
+        out, refs[:count] = refs[:count], []
+        return out
+
+    out, q, kv_out, rows_all, low_out, dwr_out, gi_out, dwo, gres, gm, vec, vec_e = take(12)
+    held, (wsems,) = take(6), take(1)
+    kv_all, low_in, far, plocal, psend, precv = take(6)
+    r1, first, r2, act_all, low_all, mixed_all, slope, local, send, recv = take(10)
+    scratch = take(11)
+    _, core, _ = places()
+    y_hi = lax.axis_index("blk_0")
+    sibling, partner = {"blk_1": 1 - core}, {"blk_0": 1 - y_hi}
+    wq, wk, wv, wo, wes, wrs = weight_loads(1, wq, wk, wv, wo, we, wr, held, wsems)
+    greet([sibling, partner])
+    project_part(1, h, early, wq, wk, wv, bq, bv, q, kv_all, rows_all, low_in, far, plocal, psend, precv)
+    copies = begin([pltpu.make_async_copy(kv_all, kv_out, local.at[0])])
+    mixed, low = mixed_all.at[core], low_all.at[core]
+    attend_part(1, (tab, cnt, two, three), q, kv_all, mixed)
+
+    def to_sibling(ref, n):
+        return begin([remote(ref, ref, send.at[n], recv.at[n], sibling)])[0]
+
+    shared = {"mixed": to_sibling(mixed, STEPS)}
+
+    def after_low():
+        shared["low"] = to_sibling(low, STEPS + 1)
+        copies.extend(begin([pltpu.make_async_copy(low, low_out.at[core], local.at[1])]))
+
+    def store(j, low_act):
+        act_all[core, j] = low_act
+        shared[j] = to_sibling(act_all.at[core, j], j)
+
+    vectors = (bo, g1, s1, be, br, g2, s2)
+    rows = pl.ds(0, ROWS)
+    result = tail_rows(1, rows, h, mixed, wo, wes, wrs, vectors, r1, first, low, slope, r2, store, after_low)
+    out[...] = result.astype(BF)
+
+    def acts(j):
+        shared[j].wait()
+        return act_all[:, j]
+
+    def mixed_pair():
+        shared["mixed"].wait()
+        return mixed_all[...]
+
+    tail_back_part(
+        1, g, lambda: r1[...], r2, acts, lambda j: slope[j], mixed_pair, None, wo, wes, wrs, g1, g2,
+        (dwr_out, gi_out, dwo, gres, gm, vec, vec_e), scratch,
+    )
+    shared["low"].wait()
+    copies += begin([pltpu.make_async_copy(low_all.at[1 - core], low_out.at[1 - core], local.at[2])])
+    end(copies)
+
+
+def second_layer(h, early, g, table, w):
+    dma, shape = pltpu.SemaphoreType.DMA, jax.ShapeDtypeStruct
+    low, full, pair = shape((ROWS, D), BF), shape((ROWS, D), F32), shape((2, ROWS, D), BF)
+    whole = pltpu.VMEM((ROWS, D), F32)
+    out, q, kv_all, rows_all, low_all, *rest = pl.pallas_call(
+        second_layer_kernel,
+        out_shape=(
+            low, low, shape((2, SLOTS * BLOCK, D), BF), shape((2, ROWS + FAR[1], D), BF), pair,
+            shape(WHOLE, BF), shape((2, ROWS, STEPS * HALF), BF), shape((D, HALF), BF), full, low,
+            shape((8, D), F32), shape((1, FF), F32),
+        ),
+        in_specs=[SMEM] * 4 + [VMEM, ANY, VMEM] + [ANY] * 6 + [VMEM] * 9,
+        out_specs=(VMEM, VMEM, ANY, ANY, ANY, ANY, ANY) + (VMEM,) * 5,
+        scratch_shapes=weight_scratch() + project_scratch(1)
+        + [whole, whole, whole, pltpu.VMEM((2, STEPS, ROWS, CHUNK), BF), pltpu.VMEM((2, ROWS, D), BF), pltpu.VMEM((2, ROWS, D), BF)]
+        + [pltpu.VMEM((STEPS, ROWS, CHUNK), BF), dma((3,)), dma((STEPS + 2,)), dma((STEPS + 2,))]
+        + tail_back_scratch(1),
+        compiler_params=pltpu.CompilerParams(collective_id=2, has_side_effects=True, vmem_limit_bytes=62 * MIB),
+        name="second_layer",
+    )(*table, h, early, g, *weight_args(w))
+    return out, dict(rows_all=rows_all, q=q, kv_all=kv_all.reshape(2, SLOTS, BLOCK, D), low_all=low_all), rest
+
+
+def tail_back_part(layer, g, r1, r2, acts, slopes, mixed_all, low_all, wo, wes, wrs, g1, g2, outs, scratch):
+    dwr_out, dwe_out, dwo, gres, gm, vec, vec_e = outs
+    dwr, dwe, go, ga, gi, gocat, gacat, gicat, local, send, recv = scratch
     core = lax.axis_index("blk_1")
     sibling = {"blk_1": 1 - core}
     mine, yours = columns_at(core * HALF, HALF), columns_at((1 - core) * HALF, HALF)
-
-    def share_go():
-        return remote(go.at[:, yours], gocat.at[core], send.at[STEPS], recv.at[STEPS], sibling)
-
-    def share_ga():
-        return remote(ga.at[:, yours], gacat.at[core], send.at[STEPS + 1], recv.at[STEPS + 1], sibling)
-
-    def share_gi(at):
-        return remote(gi.at[at, :, yours], gicat.at[at, core], send.at[at], recv.at[at], sibling)
-
-    @pl.when(j == 0)
-    def _():
-        barrier = pltpu.get_barrier_semaphore()
-        peers = [sibling] + (axis_peers((0, 1, 2)) if layer == 0 else [])
-        for peer in peers:
-            pl.semaphore_signal(barrier, inc=1, device_id=peer, device_id_type=MESH)
-        grad = g[...].astype(F32)
-        normed, inv_std = norm_parts(r2[...])
-        grad_r = norm_backward(grad, row_of(g2, layer), normed, inv_std)
-        vec[0:1] = jnp.sum(grad * normed, axis=0, keepdims=True)
-        vec[1:2] = jnp.sum(grad, axis=0, keepdims=True)
-        total[...] = grad_r
-        go[...] = grad_r.astype(BF)
-        vec[2:3] = jnp.sum(go[...].astype(F32), axis=0, keepdims=True)
-        pl.semaphore_wait(barrier, len(peers))
-        share_go().start()
-        begin(carried())
-        gocat[core] = go[:, mine]
-
-    @pl.when(j < STEPS)
-    def _():
-        grad_inner = (dot_nt(go[...], wr[...]) * slope[...].astype(F32)).astype(BF)
+    copies = []
+    grad = g[...].astype(F32)
+    normed, inv_std = norm_parts(r2[...])
+    grad_r = norm_backward(grad, row_of(g2, layer), normed, inv_std)
+    vec[0:1] = jnp.sum(grad * normed, axis=0, keepdims=True)
+    vec[1:2] = jnp.sum(grad, axis=0, keepdims=True)
+    total = grad_r
+    go[...] = grad_r.astype(BF)
+    vec[2:3] = jnp.sum(go[...].astype(F32), axis=0, keepdims=True)
+    share_go = remote(go.at[:, yours], gocat.at[core], send.at[STEPS], recv.at[STEPS], sibling)
+    share_go.start()
+    gocat[core] = go[:, mine]
+    shares = []
+
+    def expand_gradient(j):
+        shares[j].wait()
+        part = dot_tn(low_all().reshape(2 * ROWS, D), gicat[j].reshape(2 * ROWS, HALF)).astype(BF)
+        for k, piece in enumerate(pieces_of(part)):
+            dwe[k, j] = piece
+        copies.extend(begin([pltpu.make_async_copy(dwe.at[:, j], dwe_out.at[:, j], local.at[1, j])]))
+
+    for j in range(STEPS):
+        grad_inner = (dot_nt(go[...], wrs[j]()[...]) * slopes(j).astype(F32)).astype(BF)
+        gi[j] = grad_inner
         if layer == 0:
-            gi[j] = grad_inner
-            share_gi(j).start()
+            shares.append(remote(gi.at[j, :, yours], gicat.at[j, core], send.at[j], recv.at[j], sibling))
+            shares[j].start()
             gicat[j, core] = gi[j, :, mine]
         else:
-            dwe[0], dwe[1] = grad_inner[:, :HALF], grad_inner[:, HALF:]
-        vec_e[...] = jnp.sum(grad_inner.astype(F32), axis=0, keepdims=True)
-        total[...] += dot_nt(grad_inner, we[...])
-
-        @pl.when(j == 0)
-        def _():
-            share_go().wait()
-
-        grad = dot_tn(act_all[...].reshape(2 * ROWS, CHUNK), gocat[...].reshape(2 * ROWS, HALF)).astype(BF)
-        for k, piece in enumerate(pieces_of(grad)):
-            dwr[k, 0] = piece
-
-    @pl.when(j == STEPS - 1)
-    def _():
-        grad = total[...]
-        normed, inv_std = norm_parts(r1[...])
-        grad_r = norm_backward(grad, row_of(g1, layer), normed, inv_std)
-        vec[3:4] = jnp.sum(grad * normed, axis=0, keepdims=True)
-        vec[4:5] = jnp.sum(grad, axis=0, keepdims=True)
-        gres[...] = grad_r
-        ga[...] = grad_r.astype(BF)
-        vec[5:6] = jnp.sum(ga[...].astype(F32), axis=0, keepdims=True)
-        share_ga().start()
-        gacat[core] = ga[:, mine]
-
+            for half in range(2):
+                src = gi.at[j, :, pl.ds(half * HALF, HALF)]
+                dst = dwe_out.at[half, :, pl.ds(j * HALF, HALF)]
+                copies += begin([pltpu.make_async_copy(src, dst, local.at[1 + half, j])])
+        vec_e[:, j * CHUNK : (j + 1) * CHUNK] = jnp.sum(grad_inner.astype(F32), axis=0, keepdims=True)
+        total = total + dot_nt(grad_inner, wes[j]()[...])
+        if j == 0:
+            share_go.wait()
+        part = dot_tn(acts(j).reshape(2 * ROWS, CHUNK), gocat[...].reshape(2 * ROWS, HALF)).astype(BF)
+        for k, piece in enumerate(pieces_of(part)):
+            dwr[k, j] = piece
+        copies += begin([pltpu.make_async_copy(dwr.at[:, j], dwr_out.at[:, j], local.at[0, j])])
+        if layer == 0 and j > 0:
+            expand_gradient(j - 1)
+    normed, inv_std = norm_parts(r1())
+    grad_r = norm_backward(total, row_of(g1, layer), normed, inv_std)
+    vec[3:4] = jnp.sum(total * normed, axis=0, keepdims=True)
+    vec[4:5] = jnp.sum(total, axis=0, keepdims=True)
+    gres[...] = grad_r
+    ga[...] = grad_r.astype(BF)
+    vec[5:6] = jnp.sum(ga[...].astype(F32), axis=0, keepdims=True)
+    share_ga = remote(ga.at[:, yours], gacat.at[core], send.at[STEPS + 1], recv.at[STEPS + 1], sibling)
+    share_ga.start()
+    gacat[core] = ga[:, mine]
     if layer == 0:
-
-        @pl.when(j > 0)
-        def _():
-            share_gi(j - 1).wait()
-            grad = dot_tn(low_all[...].reshape(2 * ROWS, D), gicat[j - 1].reshape(2 * ROWS, HALF)).astype(BF)
-            for k, piece in enumerate(pieces_of(grad)):
-                dwe[k, 0] = piece
-
-    @pl.when(j == last)
-    def _():
-        gm[...] = dot_nt(ga[...], wo[...]).astype(BF)
-        share_ga().wait()
-        dwo[...] = dot_tn(mixed_all[...].reshape(2 * ROWS, D), gacat[...].reshape(2 * ROWS, HALF)).astype(BF)
-        end(carried())
-
-
-def tail_back(layer, g, saved, w, carry=()):
-    at = lambda j: jnp.minimum(j, STEPS - 1)
-    square = layer_block(layer, (D, D), lambda j: (0, 0))
-    wide = layer_block(layer, (D, CHUNK), lambda j: (0, at(j)))
-    tall = layer_block(layer, (CHUNK, D), lambda j: (at(j), 0))
-    full = pl.BlockSpec((ROWS, D), lambda j: (0, 0))
-    pair = pl.BlockSpec((2, ROWS, D), lambda j: (0, 0, 0))
-    vec, dma = VMEM, pltpu.SemaphoreType.DMA
-    shape = jax.ShapeDtypeStruct
-    chunk = pl.BlockSpec((3, 1) + LEFT[0], lambda j: (0, at(j), 0, 0, 0, 0))
-    if layer == 0:
-        expand, expand_spec = shape(WHOLE, BF), pl.BlockSpec((3, 1) + LEFT[0], lambda j: (0, jnp.maximum(j - 1, 0), 0, 0, 0, 0))
-    else:
-        expand, expand_spec = shape((2, ROWS, STEPS * HALF), BF), pl.BlockSpec((2, ROWS, HALF), lambda j: (0, 0, j))
+        expand_gradient(STEPS - 1)
+    gm[...] = dot_nt(ga[...], wo()[...]).astype(BF)
+    share_ga.wait()
+    dwo[...] = dot_tn(mixed_all().reshape(2 * ROWS, D), gacat[...].reshape(2 * ROWS, HALF)).astype(BF)
+    end(copies)
+
+
+def tail_back_scratch(layer):
+    dma = pltpu.SemaphoreType.DMA
+    return [
+        pltpu.VMEM(WHOLE, BF), pltpu.VMEM(WHOLE if layer == 0 else (8, 128), BF),
+        pltpu.VMEM((ROWS, D), BF), pltpu.VMEM((ROWS, D), BF), pltpu.VMEM((STEPS, ROWS, CHUNK), BF),
+        pltpu.VMEM((2, ROWS, HALF), BF), pltpu.VMEM((2, ROWS, HALF), BF),
+        pltpu.VMEM((STEPS, 2, ROWS, HALF) if layer == 0 else (8, 128), BF),
+        dma((3, STEPS)), dma((STEPS + 2,)), dma((STEPS + 2,)),
+    ]
+
+
+def tail_back_kernel(g, r1, r2, low_all, act_all, slope, mixed_all, wo, we, wr, g1, g2, q_in, e_in, *refs):
+    refs = list(refs)
+
+    def take(count):
+        out, refs[:count] = refs[:count], []
+        return out
+
+    outs, (got_q, got_e), scratch = take(7), take(2), take(11)
+    held_wr, held_slope, held_we, held_act, held_r1, held_wo, held_mixed, held_low, late, csend, crecv = take(11)
+    core = lax.axis_index("blk_1")
+    wrs, slopes, wes, acts = [], [], [], []
+    for j in range(STEPS):
+        at = chunk_columns(j)
+        wrs.append(Late(wr.at[0, at], held_wr.at[j], late.at[4 * j]))
+        slopes.append(Late(slope.at[:, at], held_slope.at[j], late.at[4 * j + 1]))
+        wes.append(Late(we.at[0, :, at], held_we.at[j], late.at[4 * j + 2]))
+        acts.append(Late(act_all.at[:, j], held_act.at[j], late.at[4 * j + 3]))
+    r1, wo = Late(r1, held_r1, late.at[4 * STEPS]), Late(wo.at[0], held_wo, late.at[4 * STEPS + 1])
+    mixed_all = Late(mixed_all, held_mixed, late.at[4 * STEPS + 2])
+    low_all = Late(low_all, held_low, late.at[4 * STEPS + 3])
+    greet([{"blk_1": 1 - core}] + axis_peers((0, 1, 2)))
+    carried = begin(stage_copies("q", 0, q_in, got_q, csend.at[0], crecv.at[0]))
+    carried += begin(stage_copies("e", 0, e_in, got_e, csend.at[1], crecv.at[1]))
+    tail_back_part(
+        0, g, lambda: r1()[...], r2, lambda j: acts[j]()[...], lambda j: slopes[j]()[...], lambda: mixed_all()[...],
+        lambda: low_all()[...], wo, wes, wrs, g1, g2, outs, scratch,
+    )
+    end(carried)
+
+
+def tail_back(g, saved, w, carry):
+    dma, shape = pltpu.SemaphoreType.DMA, jax.ShapeDtypeStruct
     return pl.pallas_call(
-        functools.partial(tail_back_kernel, layer),
-        grid=(STEPS + 1 if layer == 0 else STEPS,),
+        tail_back_kernel,
         out_shape=(
-            shape(WHOLE, BF), expand, shape((D, HALF), BF), shape((ROWS, D), F32), shape((ROWS, D), BF),
-            shape((8, D), F32), shape((1, FF), F32),
-        )
-        + ((landing(0),) * 2 if carry else ()),
-        in_specs=[
-            full, full, full, pair if layer == 0 else ANY, pl.BlockSpec((2, ROWS, CHUNK), lambda j: (0, 0, at(j))),
-            pl.BlockSpec((ROWS, CHUNK), lambda j: (0, at(j))), pair, square, wide, tall, vec, vec,
-        ]
-        + [ANY] * len(carry),
-        out_specs=(
-            chunk, expand_spec, pl.BlockSpec((D, HALF), lambda j: (0, 0)), full, full,
-            pl.BlockSpec((8, D), lambda j: (0, 0)), pl.BlockSpec((1, CHUNK), lambda j: (0, at(j))),
-        )
-        + ((ANY,) * 2 if carry else ()),
-        scratch_shapes=[
-            pltpu.VMEM((ROWS, D), BF), pltpu.VMEM((ROWS, D), BF), pltpu.VMEM((STEPS, ROWS, CHUNK), BF), pltpu.VMEM((ROWS, D), F32),
-            pltpu.VMEM((2, ROWS, HALF), BF), pltpu.VMEM((2, ROWS, HALF), BF), pltpu.VMEM((STEPS, 2, ROWS, HALF), BF),
-            dma((STEPS + 2,)), dma((STEPS + 2,)),
-        ]
-        + ([dma((2, 3, 3)), dma((2, 3, 3))] if carry else []),
-        compiler_params=pltpu.CompilerParams(collective_id=7 + layer, has_side_effects=True, vmem_limit_bytes=60 * MIB),
-        name=f"tail_back_{layer}",
+            shape(WHOLE, BF), shape(WHOLE, BF), shape((D, HALF), BF), shape((ROWS, D), F32), shape((ROWS, D), BF),
+            shape((8, D), F32), shape((1, FF), F32), landing(0), landing(0),
+        ),
+        in_specs=[VMEM, ANY, VMEM] + [ANY] * 7 + [VMEM, VMEM] + [ANY] * 2,
+        out_specs=(ANY, ANY) + (VMEM,) * 5 + (ANY,) * 2,
+        scratch_shapes=tail_back_scratch(0)
+        + [
+            pltpu.VMEM((STEPS, CHUNK, D), BF), pltpu.VMEM((STEPS, ROWS, CHUNK), BF), pltpu.VMEM((STEPS, D, CHUNK), BF),
+            pltpu.VMEM((STEPS, 2, ROWS, CHUNK), BF), pltpu.VMEM((ROWS, D), F32), pltpu.VMEM((D, D), BF),
+            pltpu.VMEM((2, ROWS, D), BF), pltpu.VMEM((2, ROWS, D), BF),
+            dma((4 * STEPS + 4,)), dma((2, 3, 3)), dma((2, 3, 3)),
+        ],
+        compiler_params=pltpu.CompilerParams(collective_id=7, has_side_effects=True, vmem_limit_bytes=60 * MIB),
+        name="tail_back_0",
     )(g, saved["r1"], saved["r2"], saved["low_all"], saved["act_all"], saved["slope"], saved["mixed_all"],
       w["output_weight"], w["expand_weight"], w["reduce_weight"], w["first_gain"], w["second_gain"], *carry)
 
@@ -1088,15 +1182,6 @@
     )(rows_all, gq, parts.reshape(2, SLOTS * BLOCK, D), gres, dwo, w["query_weight"], w["key_weight"], w["value_weight"], *carry, *vecs)
 
 
-def layer_forward(layer, h, table, w, out_type):
-    q, kv_all, rows_all = project(layer, h, w)
-    mixed = attend(layer, table, q, kv_all)
-    r1, r2, out, slope, act_all, low_all, mixed_all = tail(layer, mixed, h, w, out_type)
-    return out, dict(
-        rows_all=rows_all, q=q, kv_all=kv_all, r1=r1, r2=r2, slope=slope, act_all=act_all, low_all=low_all, mixed_all=mixed_all
-    )
-
-
 def finish_kernel(quads, rows, vecs, final, grad, *outs):
     me = lax.axis_index(DP_BLK)
     wq, wk, wv, wo, we, wr, q_b, v_b, s_g, s_s, r_b, f_g, f_s, o_b, e_b, final_out, grad_out = outs
@@ -1147,15 +1232,15 @@
 def local(hidden, output_grad, block_counts, slot_table, block_order_two, block_order_three, *weights):
     w = dict(zip(NAMES, weights))
     table = (slot_table, block_counts, block_order_two, block_order_three)
-    middle, saved_one = layer_forward(0, hidden[0], table, w, F32)
-    final, saved_two = layer_forward(1, middle, table, w, BF)
-    r_two, gi, dwo, gres, gm, vec_two, vec_e_two = tail_back(1, output_grad[0], saved_two, w)
+    middle, early, saved_one = first_layer(hidden[0], table, w)
+    final, saved_two, rest = second_layer(middle, early, output_grad[0], table, w)
+    r_two, gi, dwo, gres, gm, vec_two, vec_e_two = rest
     gq, parts, vec_p_two, gi_other, got_r = attend_back(1, table, saved_two["q"], saved_two["kv_all"], gm, gi, r_two)
     carry = (gi, gi_other, r_two, got_r)
     q_two, grad_middle, e_two, r1, got_r = project_back_two(
         saved_two["rows_all"], gq, parts, gres, dwo, w, saved_two["low_all"], carry
     )
-    r0, e0, dwo, gres, gm, vec, vec_e, got_q, got_e = tail_back(0, grad_middle, saved_one, w, (q_two, e_two))
+    r0, e0, dwo, gres, gm, vec, vec_e, got_q, got_e = tail_back(grad_middle, saved_one, w, (q_two, e_two))
     gq, parts, vec_p, got_e0, got_r0 = attend_back(0, table, saved_one["q"], saved_one["kv_all"], gm, e0, r0)
     carry = (e0, got_e0, r0, got_r0, q_two, got_q, e_two, got_e, r1, got_r)
     vecs = (vec_p, vec, vec_e, vec_p_two, vec_two, vec_e_two)

time: 269 us -> 238 us (0.88)
  Pallas kernels: 262 us -> 230 us
    pallas_call x8 -> x3, Pallas kernels: 135 us -> 108 us  [the longest x1 45.5 us: second_layer(): pl.pallas_call(second_layer_kernel, out_shape=(low, low, shape((2, SLOTS...]
where the time goes in v1:
time: 238 us; the launch traced here: 235 us
  Pallas kernels  230 us (97%)
  local copies, waits for them, and re-layouts  2.72 us (1%)
    pallas_call x1, Pallas kernels, last_step(): pl.pallas_call(last_kernel, out_shape=(shape((ROWS, D), BF), shape((2, 2,...  51.3 us
    pallas_call x1, Pallas kernels, second_layer(): pl.pallas_call(second_layer_kernel, out_shape=(low, low, shape((2, SLOTS...  45.5 us
    pallas_call x2, Pallas kernels, attend_back(): pl.pallas_call(functools.partial(attend_back_kernel, layer), grid=(HEADS...  42.7 us
    pallas_call x1, Pallas kernels, first_layer(): pl.pallas_call(first_layer_kernel, out_shape=(low, shape((2, SLOTS * BLOC...  36.5 us
    pallas_call x1, Pallas kernels, tail_back(): pl.pallas_call(tail_back_kernel, out_shape=(shape(WHOLE, BF), shape(WHOLE...  25.9 us
    pallas_call x1, Pallas kernels, project_back_two(): pl.pallas_call(project_back_two_kernel, out_shape=(shape(WHOLE, BF), shap...  25.6 us

profile of v1, /device:TPU:1, one launch (start us, length us, event | category | flops | bytes accessed | tf_op | source)
XLA Modules:
  0.0 234.8 jit_solution(14839919764530087625)
XLA Ops:
  1.3 1.4 copy.38.two
  2.7 1.4 copy.39.three
  4.0 36.5 %first_layer.1 = (bf16[384,768]{1,0:T(8,128)(2,1)}, bf16[2,1536,768]{2,1,0:T(8,128)(2,1)}, bf16[2,640,768]{2,1,0:T(8,128)(2,1)}, f32[384,768]{1,0:T(8,128)}, f32...) custom-call(s32[1,3]{1,0:T(1,128)} %tab.7, ...), custom_call_target="tpu_custom_call" | custom-call | tf_op jit(solution)/shard_map/first_layer/pallas_call | solution.py:736
  40.6 45.5 %second_layer.1 = (bf16[384,768]{1,0:T(8,128)(2,1)}, bf16[384,768]{1,0:T(8,128)(2,1)}, bf16[2,1536,768]{2,1,0:T(8,128)(2,1)}, bf16[2,768,768]{2,1,0:T(8,128)(2,1...) custom-call(s32[1,3]{1,0:T(1,128)} %tab.7, ...), custom_call_target="tpu_custom_call" | custom-call | tf_op jit(solution)/shard_map/second_layer/pallas_call | solution.py:819
  86.1 19.0 %attend_back_1.1 = (bf16[384,768]{1,0:T(8,128)(2,1)}, bf16[2,3,512,768]{3,2,1,0:T(8,128)(2,1)}, f32[2,768]{1,0:T(2,128)}, bf16[384,1536]{1,0:T(8,128)(2,1)}, bf16[3,3,4,4,48,128]{5,4,3,2,1,0:T(8,128)(2,1)}) custom-call(s32[1,3]{1,0:T(1,128)} %tab.7, s32[1]{0:T(128)S(6)} %copy.46.cnt, s32[12,2]{1,0:T(8,128)} %copy.38.two, s32[12,3]{1,0:T(8,128)} %copy.39.three, ...), custom_call_target="tpu_custom_call" | custom-call | tf_op jit(solution)/shard_map/attend_back_1/pallas_call | solution.py:538
  105.1 25.6 %project_back_1.1 = (bf16[3,4,4,4,48,128]{5,4,3,2,1,0:T(8,128)(2,1)}, f32[384,768]{1,0:T(8,128)}, bf16[3,4,4,4,48,128]{5,4,3,2,1,0:T(8,128)(2,1)}, bf16[3,4,4,48...) custom-call(bf16[2,768,768]{2,1,0:T(8,128)(2,1)} %get-tuple-element.90.rows, bf16[384,768]{1,0:T(8,128)(2,1)} %get-tuple-element.96.gq, ...), custom_call_target="tpu_custom_call" | custom-call | tf_op jit(solution)/shard_map/project_back_1/pallas_call | solution.py:393
  130.7 25.9 %tail_back_0.1 = (bf16[3,4,4,4,48,128]{5,4,3,2,1,0:T(8,128)(2,1)}, bf16[3,4,4,4,48,128]{5,4,3,2,1,0:T(8,128)(2,1)}, bf16[768,384]{1,0:T(8,128)(2,1)}, f32[384,76...) custom-call(f32[384,768]{1,0:T(8,128)} %get-tuple-element.103.g, ...), custom_call_target="tpu_custom_call" | custom-call | tf_op jit(solution)/shard_map/tail_back_0/pallas_call | solution.py:948
  156.6 23.7 %attend_back_0.1 = (bf16[384,768]{1,0:T(8,128)(2,1)}, bf16[2,3,512,768]{3,2,1,0:T(8,128)(2,1)}, f32[2,768]{1,0:T(2,128)}, bf16[3,3,4,4,48,128]{5,4,3,2,1,0:T(8,128)(2,1)}, bf16[3,3,4,4,48,128]{5,4,3,2,1,0:T(8,128)(2,1)}) custom-call(s32[1,3]{1,0:T(1,128)} %tab.7, s32[1]{0:T(128)S(6)} %copy.46.cnt, s32[12,2]{1,0:T(8,128)} %copy.38.two, s32[12,3]{1,0:T(8,128)} %copy.39.three, ...), custom_call_target="tpu_custom_call" | custom-call | tf_op jit(solution)/shard_map/attend_back_0/pallas_call | solution.py:538
  180.3 51.3 %last_step.1 = (bf16[384,768]{1,0:T(8,128)(2,1)}, f32[2,2,8,8,384]{4,3,2,1,0:T(8,128)}, f32[2,2,24,384]{3,2,1,0:T(8,128)}, f32[8,8,768]{2,1,0:T(8,128)}) custom-call(bf16[2,640,768]{2,1,0:T(8,128)(2,1)} %get-tuple-element.85.refs_0_, bf16[384,768]{1,0:T(8,128)(2,1)} %get-tuple-element.115.refs_1_, bf16[2,1536,768]{2,1,0:T(8,128)(2,1)} %bitcast.17, ...), custom_call_target="tpu_custom_call" | custom-call | tf_op jit(solution)/shard_map/last_step/pallas_call | solution.py:1161
  231.7 2.8 %finish.1 = (f32[6,2,768]{2,1,0:T(2,128)}, f32[6,2,768]{2,1,0:T(2,128)}, f32[6,2,768]{2,1,0:T(2,128)}, f32[6,2,768]{2,1,0:T(2,128)}, f32[6,2,3072]{2,1,0:T(2,128...) custom-call(f32[2,2,8,8,384]{4,3,2,1,0:T(8,128)} %get-tuple-element., ...), custom_call_target="tpu_custom_call" | custom-call | tf_op jit(solution)/shard_map/finish/pallas_call | solution.py:1213

commit v2 on v1

--- a/solution.py
+++ b/solution.py
@@ -109,28 +109,30 @@
 
 
 def add_up(own, got, out, streams=3):
-    count = out.shape[1] * out.shape[2] if len(out.shape) == 5 else out.shape[1]
     for n in range(streams):
 
-        @pl.loop(0, count)
-        def _(k, n=n):
-            at = (k // 4, lax.rem(k, 4)) if len(out.shape) == 5 else (k,)
+        def part(at, n=n):
             total = own[n](at).astype(F32)
             for d in range(3):
                 total += got[(n, d) + at].astype(F32)
             out[(n,) + at] = total.astype(out.dtype)
 
+        if len(out.shape) == 5:
+            pl.loop(0, 4)(lambda k, part=part: part((k,)))
+        else:
+            part((slice(None),))
+
 
 def chip_place():
     y = lax.axis_index("blk_0") * 2 + lax.axis_index("dp_2")
     return (lax.axis_index("dp_0"), lax.axis_index("dp_1"), y)
 
 
-def stage_copies(group, stage, source, got, send, recv):
+def stage_copies(group, stage, source, got, send, recv, streams=(0, 1, 2)):
     place = chip_place()
     copies = []
     for d in (2, 1, 3):
-        for n in range(3):
+        for n in streams:
             axis = STREAM_ORDERS[n][stage]
             src = share(group, stage, n, source, lax.rem(place[axis] + d, 4))
             copies.append(remote(src, got.at[n, d - 1], send.at[n, d - 1], recv.at[n, d - 1], peer_of(axis, place, d)))
@@ -210,11 +212,11 @@
     return pl.ds(pl.multiple_of(start, PIECE), count)
 
 
-def greet(devices):
+def hail(devices):
     barrier = pltpu.get_barrier_semaphore()
     for device in devices:
         pl.semaphore_signal(barrier, inc=1, device_id=device, device_id_type=MESH)
-    pl.semaphore_wait(barrier, len(devices))
+    return lambda: pl.semaphore_wait(barrier, len(devices))
 
 
 FAR = (256, ROWS)
@@ -232,11 +234,9 @@
     return jnp.logical_and(block >= 1, block <= 2)
 
 
-def project_back_body(layer, rows, gq, parts, gres, dwo, wq, wk, wv, p0, gh, scratch, peers, hooks):
-    (
-        grads, near, far_near, gh_send, gh_got, qcat, kvcat, local, send, recv,
-        held_rows, held_gq, held_gres, held_dwo, held_q, held_k, held_v, late,
-    ) = scratch
+def project_back_body(layer, rows, gq, parts, arrived, gres, dwo, weights, p0, gh, scratch, hooks):
+    grads, near, far_near, gh_send, gh_got, qcat, kvcat, send, recv = scratch
+    wq, wk, wv = weights
     y_hi, core, block = places()
     far_rows = FAR[layer]
     sibling = {"blk_1": 1 - core}
@@ -244,75 +244,49 @@
     mine = columns_at(core * HALF, HALF)
     yours = columns_at((1 - core) * HALF, HALF)
 
-    def hook(name):
-        if name in hooks:
-            hooks[name]()
-
     def talk(step):
         if layer == 0:
             pl.when(is_middle(block))(step)
         else:
             step()
 
-    own = begin(
-        [
-            pltpu.make_async_copy(parts.at[:, rows_at(theirs, far_rows)], grads.at[:, pl.ds(ROWS, far_rows)], local.at[0]),
-            pltpu.make_async_copy(parts.at[:, rows_at(block * ROWS, ROWS)], grads.at[:, pl.ds(0, ROWS)], local.at[1]),
-            pltpu.make_async_copy(gq.at[:, mine], qcat.at[core], local.at[2]),
-        ]
-    )
-    wk, wv = Late(wk.at[layer], held_k, late.at[0]), Late(wv.at[layer], held_v, late.at[1])
-    dwo, rows = Late(dwo, held_dwo, late.at[2]), Late(rows, held_rows, late.at[3])
-    gq_held, wq = Late(gq, held_gq, late.at[4]), Late(wq.at[layer], held_q, late.at[5])
-    gres = Late(gres, held_gres, late.at[6])
-    hook("loads")
-    greet(peers or [sibling, partner] + axis_peers((0, 1, 2), (1, 2, 3)))
-    beside = y_hi * 2 + 1 - core
-    copies = []
+    half_q = remote(gq.at[:, yours], qcat.at[core], send.at[1], recv.at[1], sibling)
+    half_q.start()
+    end(arrived)
+    far = parts[:, rows_at(theirs, far_rows)]
     if layer == 1:
-        at = (1 - y_hi) * 2 + 1 - core
-        copies.append(remote(parts.at[:, rows_at(at * ROWS, ROWS)], far_near, send.at[0], recv.at[0], sibling))
-    copies.append(remote(parts.at[:, rows_at(beside * ROWS, ROWS)], near, send.at[1], recv.at[1], sibling))
-    half_q = remote(gq.at[:, yours], qcat.at[core], send.at[3], recv.at[3], sibling)
-    begin(copies + [half_q])
-    hook("greeted")
+        far = (far.astype(F32) + far_near[...].astype(F32)).astype(BF)
+    grads[:, ROWS:] = far
+    wk(), wv()
+    hidden = remote(gh_send, gh_got, send.at[0], recv.at[0], partner)
+
+    def far_part():
+        gh_send[...] = (dot_nt(grads[0, ROWS:], wk()[...]) + dot_nt(grads[1, ROWS:], wv()[...])).astype(BF)
+        hidden.start()
+
+    talk(far_part)
+    hooks["far"]()
+    grads[:, 0:ROWS] = (parts[:, rows_at(block * ROWS, ROWS)].astype(F32) + near[...].astype(F32)).astype(BF)
+    half_kv = remote(grads.at[:, :, yours], kvcat.at[:, core], send.at[2], recv.at[2], sibling)
+    half_kv.start()
+    qcat[core] = gq[:, mine]
+    kvcat[:, core] = grads[:, :, mine]
 
     def place_square(y, grad):
         for k, piece in enumerate(pieces_of(grad)):
             p0[k, y] = piece
 
-    own[0].wait()
-    wk(), wv()
-    if layer == 1:
-        copies[0].wait()
-        grads[:, ROWS:] = (grads[:, ROWS:].astype(F32) + far_near[...].astype(F32)).astype(BF)
-    hidden = remote(gh_send, gh_got, send.at[2], recv.at[2], partner)
-
-    def far_part():
-        gh_send[...] = (dot_nt(grads[0, ROWS:], wk()[...]) + dot_nt(grads[1, ROWS:], wv()[...])).astype(BF)
-        hidden.start()
-
-    talk(far_part)
-    hook("far")
-    own[1].wait()
-    copies[-1].wait()
-    grads[:, 0:ROWS] = (grads[:, 0:ROWS].astype(F32) + near[...].astype(F32)).astype(BF)
-    half_kv = remote(grads.at[:, :, yours], kvcat.at[:, core], send.at[4], recv.at[4], sibling)
-    half_kv.start()
-    kvcat[:, core] = grads[:, :, mine]
-    hook("near")
     place_square(1, dwo()[...])
-    own[2].wait()
     half_q.wait()
     rows = rows()
     place_square(0, (dot_tn(rows[0, 0:ROWS], qcat[0]) + dot_tn(rows[1, 0:ROWS], qcat[1])).astype(BF))
-    hook("two_squares")
+    hooks["two_squares"]()
     half_kv.wait()
     for side in (0, 1):
         cat = kvcat[side].reshape(2 * (ROWS + far_rows), HALF)
         place_square(2 + side, dot_tn(rows[...].reshape(2 * (ROWS + far_rows), D), cat).astype(BF))
-    hook("squares")
-    total = gres()[...] + dot_nt(gq_held()[...], wq()[...])
+    hooks["squares"]()
+    total = gres()[...] + dot_nt(gq[...], wq()[...])
     total += dot_nt(grads[0, 0:ROWS], wk()[...]) + dot_nt(grads[1, 0:ROWS], wv()[...])
     if layer == 1:
         hidden.wait()
@@ -329,14 +303,26 @@
 
 def project_back_scratch(layer):
     far_rows, dma = FAR[layer], pltpu.SemaphoreType.DMA
+    across = (2, far_rows, D) if layer == 1 else (8, 128)
     return [
         pltpu.VMEM((2, ROWS + far_rows, D), BF), pltpu.VMEM((2, ROWS, D), BF),
-        pltpu.VMEM((2, far_rows, D), BF), pltpu.VMEM((far_rows, D), BF), pltpu.VMEM((far_rows, D), BF),
+        pltpu.VMEM(across, BF), pltpu.VMEM((far_rows, D), BF), pltpu.VMEM((far_rows, D), BF),
         pltpu.VMEM((2, ROWS, HALF), BF), pltpu.VMEM((2, 2, ROWS + far_rows, HALF), BF),
-        dma((3,)), dma((5,)), dma((5,)),
-        pltpu.VMEM((2, ROWS + far_rows, D), BF), pltpu.VMEM((ROWS, D), BF), pltpu.VMEM((ROWS, D), F32), pltpu.VMEM((D, HALF), BF),
-        pltpu.VMEM((D, D), BF), pltpu.VMEM((D, D), BF), pltpu.VMEM((D, D), BF), dma((7,)),
+        dma((3,)), dma((3,)),
     ]
+
+
+def operand_scratch(layer):
+    return [
+        pltpu.VMEM((D, D), BF), pltpu.VMEM((D, D), BF), pltpu.VMEM((D, D), BF), pltpu.VMEM((2, ROWS + FAR[layer], D), BF),
+        pltpu.VMEM((ROWS, D), F32), pltpu.VMEM((D, HALF), BF), pltpu.SemaphoreType.DMA((6,)),
+    ]
+
+
+def operand_loads(layer, wq, wk, wv, rows, gres, dwo, held):
+    sems = held[-1]
+    sources = (wq.at[layer], wk.at[layer], wv.at[layer], rows, gres, dwo)
+    return [Late(source, into, sems.at[n]) for n, (source, into) in enumerate(zip(sources, held))]
 
 
 def own_scratch(stage):
@@ -347,61 +333,77 @@
     return pltpu.VMEM((3, 3) + LEFT[stage], BF)
 
 
-def project_back_two_kernel(
-    rows, gq, parts, gres, dwo, wq, wk, wv, low_all, gi, gi_other, r0, got_r0, p0_out, gh, e_out, s_r, got_r, *refs
+def second_back_kernel(
+    tab, cnt, two, three, q, kv, gm, gi, r0, low_all, rows, gres, dwo, wq, wk, wv, p0_out, gh, e_out, s_r, got_r, vec, got_e, *refs
 ):
-    scratch, (p0, e, gicat, held_low, own_r, held_r, csems, gsems, osems, csend, crecv) = refs[:18], refs[18:]
+    refs = list(refs)
+
+    def take(count):
+        out, refs[:count] = refs[:count], []
+        return out
+
+    held_q, held_kv, held_gm, gq, parts, acc, asems, asend, arecv = take(9)
+    scratch, held = take(9), take(7)
+    p0, e, gicat, held_low, own_r, held_r, csems, gsems, osems, rsend, rrecv, csend, crecv, esend, erecv = take(15)
     core = lax.axis_index("blk_1")
-    loads_g, loads_r, carried = [], [], []
-
-    def loads():
-        loads_r.extend(begin(own_loads("r", 0, r0, own_r, got_r0, held_r, csems)))
-        loads_g.extend(
-            begin(
-                [
-                    pltpu.make_async_copy(gi.at[core], gicat.at[core], gsems.at[0]),
-                    pltpu.make_async_copy(gi_other, gicat.at[1 - core], gsems.at[1]),
-                    pltpu.make_async_copy(low_all, held_low, gsems.at[2]),
-                ]
-            )
-        )
+    table = (tab, cnt, two, three)
+    met = hail([{"blk_1": 1 - core}] + axis_peers((0, 1, 2)))
+    first = begin(
+        [pltpu.make_async_copy(src, dst, asems.at[n]) for n, (src, dst) in enumerate(((q, held_q), (kv, held_kv), (gm, held_gm)))]
+    )
+    *weights, rows, gres, dwo = operand_loads(1, wq, wk, wv, rows, gres, dwo, held)
+    loads = begin(
+        [
+            pltpu.make_async_copy(gi, gicat, gsems.at[0]),
+            pltpu.make_async_copy(low_all, held_low, gsems.at[1]),
+        ]
+    )
+    own_loads_r = begin([pltpu.make_async_copy(own_share("r", 0, n, r0), own_r.at[n], csems.at[n]) for n in range(3)])
+    end(loads)
+    for y in (0, 2):
+        both = gicat[:, :, y * HALF : (y + 2) * HALF].reshape(2 * ROWS, 2 * HALF)
+        grad = dot_tn(held_low[...].reshape(2 * ROWS, D), both).astype(BF)
+        for k, piece in enumerate(pieces_of(grad[:, :HALF])):
+            e[k, y] = piece
+        for k, piece in enumerate(pieces_of(grad[:, HALF:])):
+            e[k, y + 1] = piece
+    met()
+    travelling = begin(stage_copies("r", 0, r0, held_r, rsend, rrecv))
+    carried = begin(stage_copies("e", 0, e, got_e, esend, erecv))
+    carried += begin([pltpu.make_async_copy(e, e_out, osems.at[0])])
+    end(first)
+    arrived = attend_back_part(1, table, held_q, held_kv, held_gm, gq, parts, vec, acc, scratch[1], scratch[2], asend, arecv)
 
     def two_squares():
-        end(loads_r)
+        end(own_loads_r + travelling)
         add_held(own_r, held_r, s_r)
         carried.extend(begin(stage_copies("r", 1, s_r, got_r, csend, crecv)))
-        end(loads_g)
-        for y in (0, 2):
-            both = gicat[:, :, y * HALF : (y + 2) * HALF].reshape(2 * ROWS, 2 * HALF)
-            grad = dot_tn(held_low[...].reshape(2 * ROWS, D), both).astype(BF)
-            for k, piece in enumerate(pieces_of(grad[:, :HALF])):
-                e[k, y] = piece
-            for k, piece in enumerate(pieces_of(grad[:, HALF:])):
-                e[k, y + 1] = piece
-        carried.extend(begin([pltpu.make_async_copy(e, e_out, osems.at[0])]))
 
     def squares():
         carried.extend(begin([pltpu.make_async_copy(p0, p0_out, osems.at[1])]))
 
-    hooks = dict(loads=loads, two_squares=two_squares, squares=squares)
-    project_back_body(1, rows, gq, parts, gres, dwo, wq, wk, wv, p0, gh, scratch, None, hooks)
+    hooks = dict(far=lambda: None, two_squares=two_squares, squares=squares)
+    project_back_body(1, rows, gq, parts, arrived, gres, dwo, weights, p0, gh, scratch, hooks)
     end(carried)
 
 
-def project_back_two(rows_all, gq, parts, gres, dwo, w, low_all, carry):
+def second_back(table, saved, gm, gi, r0, gres, dwo, w):
     shape, dma = jax.ShapeDtypeStruct, pltpu.SemaphoreType.DMA
     return pl.pallas_call(
-        project_back_two_kernel,
-        out_shape=(shape(WHOLE, BF), shape((ROWS, D), F32), shape(WHOLE, BF), shape(summed(0), BF), landing(1)),
-        in_specs=[ANY] * 13,
-        out_specs=(ANY, VMEM, ANY, VMEM, ANY),
-        scratch_shapes=project_back_scratch(1)
+        second_back_kernel,
+        out_shape=(
+            shape(WHOLE, BF), shape((ROWS, D), F32), shape(WHOLE, BF), shape(summed(0), BF), landing(1), shape((2, D), F32),
+            landing(0),
+        ),
+        in_specs=[SMEM] * 4 + [ANY] * 12,
+        out_specs=(ANY, VMEM, ANY, VMEM, ANY, VMEM, ANY),
+        scratch_shapes=attend_back_scratch() + project_back_scratch(1) + operand_scratch(1)
         + [pltpu.VMEM(WHOLE, BF), pltpu.VMEM(WHOLE, BF), pltpu.VMEM((2, ROWS, STEPS * HALF), BF), pltpu.VMEM((2, ROWS, D), BF)]
-        + [own_scratch(0), got_scratch(0), dma((4,)), dma((3,)), dma((2,)), dma((3, 3)), dma((3, 3))],
+        + [own_scratch(0), got_scratch(0), dma((3,)), dma((2,)), dma((2,))] + [dma((3, 3))] * 6,
         compiler_params=pltpu.CompilerParams(collective_id=4, has_side_effects=True, vmem_limit_bytes=60 * MIB),
-        name="project_back_1",
-    )(rows_all, gq, parts.reshape(2, SLOTS * BLOCK, D), gres, dwo, w["query_weight"], w["key_weight"], w["value_weight"],
-      low_all, *carry)
+        name="second_back",
+    )(*table, saved["q"], saved["kv_all"], gm, gi, r0, saved["low_all"], saved["rows_all"], gres, dwo,
+      w["query_weight"], w["key_weight"], w["value_weight"])
 
 
 def slots_of(layer, tab, cnt, two, three, piece, head):
@@ -411,8 +413,8 @@
     live = jnp.where(j < cnt[0], 1.0, 0.0)
     if layer == 0:
         return t, live
-    from_two = jnp.where(j < 2, two[head, jnp.minimum(j, 1)], j)
-    chosen = jnp.where(cnt[0] == SLOTS, three[head, j], from_two)
+    from_two = jnp.where(j < 2, two[jnp.minimum(j, 1), head], j)
+    chosen = jnp.where(cnt[0] == SLOTS, three[j, head], from_two)
     return tab[0, chosen], live
 
 
@@ -439,31 +441,22 @@
     return jnp.where(left_lanes(), first, second).astype(kind)
 
 
-def attend_specs():
-    tile = pl.BlockSpec((ROWS, 2 * HD), lambda p: (0, p))
-    keys = pl.BlockSpec((None, SLOTS, BLOCK, 2 * HD), lambda p: (0, 0, 0, p))
-    values = pl.BlockSpec((None, SLOTS, BLOCK, 2 * HD), lambda p: (1, 0, 0, p))
-    return tile, keys, values
-
-
-def attend_back_step(layer, tab, cnt, two, three, q, k, v, gm, gq, gkv, acc):
-    pair = pl.program_id(0)
+def attend_back_step(layer, table, pair, columns, q, kv, gm, gq, parts, acc):
     masks = []
     if layer == 0:
         acc[...] = jnp.zeros_like(acc)
     for i in range(3):
         rows = pl.ds(i * PIECE, PIECE)
-        s0, live = slots_of(layer, tab, cnt, two, three, i, 2 * pair)
+        s0, live = slots_of(layer, *table, i, 2 * pair)
         if layer == 0:
-            keys, values = k[s0], v[s0]
+            keys, values = kv[0, s0, :, columns], kv[1, s0, :, columns]
         else:
-            s1, _ = slots_of(layer, tab, cnt, two, three, i, 2 * pair + 1)
+            s1, _ = slots_of(layer, *table, i, 2 * pair + 1)
             low = [slot_mask(s0, s1, t, BF) for t in range(SLOTS)]
             masks.append([slot_mask(s0, s1, t, F32) for t in range(SLOTS)])
-            keys = k[0] * low[0] + k[1] * low[1] + k[2] * low[2]
-            values = v[0] * low[0] + v[1] * low[1] + v[2] * low[2]
-        qq = two_heads(q[rows, :] * jnp.asarray(SCALE, BF))
-        gg = two_heads((gm[rows, :].astype(F32) * live).astype(BF))
+            keys, values = [sum(kv[side, t, :, columns] * low[t] for t in range(SLOTS)) for side in (0, 1)]
+        qq = two_heads(q[rows, columns] * jnp.asarray(SCALE, BF))
+        gg = two_heads((gm[rows, columns].astype(F32) * live).astype(BF))
         scores = dot_nt(keys, qq)
         exps = jnp.exp(scores - jnp.max(scores, axis=0, keepdims=True))
         factor = 1.0 / jnp.sum(exps, axis=0, keepdims=True)
@@ -471,7 +464,7 @@
         delta = jnp.sum(exps * grad_weights, axis=0, keepdims=True) * factor
         weights = exps * factor
         grad_scores = (weights * (grad_weights - delta)).astype(BF)
-        gq[rows, :] = (own_rows(dot_tn(keys, grad_scores)) * SCALE).astype(BF)
+        gq[rows, columns] = (own_rows(dot_tn(keys, grad_scores)) * SCALE).astype(BF)
         gk = dot(grad_scores, qq)
         gv = dot(weights.astype(BF), gg)
         if layer == 0:
@@ -481,70 +474,71 @@
             acc[0, i] = gk
             acc[1, i] = gv
     if layer == 0:
-        gkv[...] = acc[...].astype(BF)
+        parts[:, :, columns] = acc[...].reshape(2, SLOTS * BLOCK, 2 * HD).astype(BF)
     else:
         for side in range(2):
             for t in range(SLOTS):
                 total = acc[side, 0] * masks[0][t] + acc[side, 1] * masks[1][t] + acc[side, 2] * masks[2][t]
-                gkv[side, t] = total.astype(BF)
-
-
-def attend_back_kernel(layer, tab, cnt, two, three, q, k, v, gm, e, r, gq, gkv, vec, got_e, got_r, acc, send, recv):
-    step = pl.program_id(0)
-    core = lax.axis_index("blk_1")
-
-    def carried():
-        copies = stage_copies("r", 0, r, got_r, send.at[0], recv.at[0])
-        if layer == 0:
-            return copies + stage_copies("e", 0, e, got_e, send.at[1], recv.at[1])
-        return copies + [remote(e.at[1 - core], got_e, send.at[1, 0, 0], recv.at[1, 0, 0], {"blk_1": 1 - core})]
-
-    peers = axis_peers((0, 1, 2)) + ([{"blk_1": 1 - core}] if layer == 1 else [])
-
-    @pl.when(step == 0)
-    def _():
-        barrier = pltpu.get_barrier_semaphore()
-        for peer in peers:
-            pl.semaphore_signal(barrier, inc=1, device_id=peer, device_id_type=MESH)
-        if layer == 0:
-            pl.semaphore_wait(barrier, len(peers))
-            begin(carried())
-
-    attend_back_step(layer, tab, cnt, two, three, q, k, v, gm, gq, gkv, acc)
+                parts[side, t * BLOCK : (t + 1) * BLOCK, columns] = total.astype(BF)
+
+
+def attend_back_part(layer, table, q, kv, gm, gq, parts, vec, acc, near, far_near, send, recv, halves=None):
+    y_hi, core, _ = places()
+    sibling = {"blk_1": 1 - core}
+
+    def share(pair):
+        columns = columns_at(pair * 2 * HD, 2 * HD)
+        beside = rows_at((y_hi * 2 + 1 - core) * ROWS, ROWS)
+        out = [remote(parts.at[:, beside, columns], near.at[:, :, columns], send.at[0, pair], recv.at[0, pair], sibling)]
+        if layer == 1:
+            across = rows_at(((1 - y_hi) * 2 + 1 - core) * ROWS, ROWS)
+            out.append(
+                remote(parts.at[:, across, columns], far_near.at[:, :, columns], send.at[1, pair], recv.at[1, pair], sibling)
+            )
+        return out
+
+    def half_copies(i):
+        theirs, hsend, hrecv = halves
+        columns, to = columns_at(((1 - core) * 3 + i) * 2 * HD, 2 * HD), columns_at(i * 2 * HD, 2 * HD)
+        out = []
+        for n, (start, count, at) in enumerate(((y_hi * 2 * ROWS, 2 * ROWS, 0), (far_start(y_hi), FAR[0], 2 * ROWS))):
+            src, dst = parts.at[:, rows_at(start, count), columns], theirs.at[:, pl.ds(at, count), to]
+            out.append(remote(src, dst, hsend.at[n, i], hrecv.at[n, i], sibling))
+        return out
+
+    @pl.loop(0, HEADS // 2)
+    def _(pair):
+        columns = columns_at(pair * 2 * HD, 2 * HD)
+        attend_back_step(layer, table, pair, columns, q, kv, gm, gq, parts, acc)
+        if halves:
+
+            @pl.when(pair // 3 == 1 - core)
+            def _():
+                begin(half_copies(lax.rem(pair, 3)))
+
+        begin(share(pair))
+
     vec[0:1] = jnp.sum(gq[...].astype(F32), axis=0, keepdims=True)
-    total = jnp.zeros((1, 2 * HD), F32)
+    total = jnp.zeros((1, D), F32)
     for i in range(3):
-        _, live = slots_of(0, tab, cnt, two, three, i, 0)
+        _, live = slots_of(0, *table, i, 0)
         total += live * jnp.sum(gm[i * PIECE : (i + 1) * PIECE, :].astype(F32), axis=0, keepdims=True)
     vec[1:2] = total
-
-    if layer == 1:
-
-        @pl.when(step == 0)
-        def _():
-            pl.semaphore_wait(pltpu.get_barrier_semaphore(), len(peers))
-            begin(carried())
-
-    @pl.when(step == HEADS // 2 - 1)
-    def _():
-        end(carried())
-
-
-def attend_back(layer, table, q, kv_all, gm, e, r):
-    tile, keys, values = attend_specs()
-    both = pl.BlockSpec((2, SLOTS, BLOCK, 2 * HD), lambda p: (0, 0, 0, p))
-    shape, dma = jax.ShapeDtypeStruct, pltpu.SemaphoreType.DMA
-    landed = landing(0) if layer == 0 else shape((ROWS, STEPS * HALF), BF)
-    return pl.pallas_call(
-        functools.partial(attend_back_kernel, layer),
-        grid=(HEADS // 2,),
-        out_shape=(shape((ROWS, D), BF), shape((2, SLOTS, BLOCK, D), BF), shape((2, D), F32), landed, landing(0)),
-        in_specs=[SMEM] * 4 + [tile, keys, values, tile, ANY, ANY],
-        out_specs=(tile, both, pl.BlockSpec((2, 2 * HD), lambda p: (0, p)), ANY, ANY),
-        scratch_shapes=[pltpu.VMEM((2, SLOTS, BLOCK, 2 * HD), F32), dma((2, 3, 3)), dma((2, 3, 3))],
-        compiler_params=pltpu.CompilerParams(collective_id=9 + layer, has_side_effects=True, vmem_limit_bytes=60 * MIB),
-        name=f"attend_back_{layer}",
-    )(*table, q, kv_all, kv_all, gm, e, r)
+    arrived = [c for pair in range(HEADS // 2) for c in share(pair)]
+    return (arrived, [c for i in range(3) for c in half_copies(i)]) if halves else arrived
+
+
+def far_start(y_hi):
+    return (1 - y_hi) * 256 + 512
+
+
+def attend_back_scratch():
+    dma = pltpu.SemaphoreType.DMA
+    return [
+        pltpu.VMEM((ROWS, D), BF), pltpu.VMEM((2, SLOTS, BLOCK, D), BF), pltpu.VMEM((ROWS, D), BF), pltpu.VMEM((ROWS, D), BF),
+        pltpu.VMEM((2, SLOTS * BLOCK, D), BF), pltpu.VMEM((2, SLOTS, BLOCK, 2 * HD), F32),
+        dma((3,)), dma((2, HEADS // 2)), dma((2, HEADS // 2)),
+    ]
 
 
 STEPS = FF // CHUNK
@@ -575,7 +569,7 @@
         there = pltpu.make_async_copy(early, far.at[pl.ds(0, EARLY)], local.at[0])
         there.start()
     own_dst = rows_all.at[core, pl.ds(0, ROWS)]
-    copies = begin([remote(low, own_dst, send.at[1], recv.at[1], sibling), pltpu.make_async_copy(low, own_dst, local.at[1])])
+    copies, kept = [], begin([remote(low, own_dst, send.at[1], recv.at[1], sibling), pltpu.make_async_copy(low, own_dst, local.at[1])])
 
     def keys_of(source, count, start):
         at = rows_at(start, count) if count % PIECE == 0 else pl.ds(pl.multiple_of(start, 64), count)
@@ -598,13 +592,14 @@
             far[...] = jnp.zeros_like(far)
 
     far_dst = rows_all.at[core, pl.ds(ROWS, far_rows)]
-    copies += begin([remote(far, far_dst, send.at[4], recv.at[4], sibling), pltpu.make_async_copy(far, far_dst, local.at[2])])
+    kept += begin([remote(far, far_dst, send.at[4], recv.at[4], sibling), pltpu.make_async_copy(far, far_dst, local.at[2])])
     if layer == 0:
         talk(lambda: keys_of(far[...], far_rows, theirs) and None)
     else:
         part = keys_of(far[first:far_rows], far_rows - first, theirs + first)
         copies += begin([remote(part, part, send.at[5], recv.at[5], sibling)])
     end(copies)
+    return kept
 
 
 def attend_part(layer, table, q, kv_all, mixed):
@@ -686,10 +681,11 @@
     mixed, r1, first, low, act, slope, next_low, local, send, recv = take(10)
     y_hi, core, _ = places()
     sibling, partner = {"blk_1": 1 - core}, {"blk_0": 1 - y_hi}
+    met = hail([sibling, partner, {"blk_0": 1 - y_hi, "blk_1": 1 - core}])
     wq, wk, wv, wo, wes, wrs = weight_loads(0, wq, wk, wv, wo, we, wr, held, wsems)
-    greet([sibling, partner, {"blk_0": 1 - y_hi, "blk_1": 1 - core}])
-    project_part(0, h, None, wq, wk, wv, bq, bv, q, kv_all, rows_all, low_in, far, plocal, psend, precv)
-    copies = begin([pltpu.make_async_copy(kv_all, kv_out, local.at[2 * STEPS + 3])])
+    met()
+    kept = project_part(0, h, None, wq, wk, wv, bq, bv, q, kv_all, rows_all, low_in, far, plocal, psend, precv)
+    copies = kept + begin([pltpu.make_async_copy(kv_all, kv_out, local.at[2 * STEPS + 3])])
     attend_part(0, (tab, cnt, two, three), q, kv_all, mixed)
 
     def both(src, dst, n):
@@ -770,10 +766,11 @@
     _, core, _ = places()
     y_hi = lax.axis_index("blk_0")
     sibling, partner = {"blk_1": 1 - core}, {"blk_0": 1 - y_hi}
+    met = hail([sibling, partner])
     wq, wk, wv, wo, wes, wrs = weight_loads(1, wq, wk, wv, wo, we, wr, held, wsems)
-    greet([sibling, partner])
-    project_part(1, h, early, wq, wk, wv, bq, bv, q, kv_all, rows_all, low_in, far, plocal, psend, precv)
-    copies = begin([pltpu.make_async_copy(kv_all, kv_out, local.at[0])])
+    met()
+    kept = project_part(1, h, early, wq, wk, wv, bq, bv, q, kv_all, rows_all, low_in, far, plocal, psend, precv)
+    copies = kept + begin([pltpu.make_async_copy(kv_all, kv_out, local.at[0])])
     mixed, low = mixed_all.at[core], low_all.at[core]
     attend_part(1, (tab, cnt, two, three), q, kv_all, mixed)
 
@@ -835,7 +832,11 @@
     return out, dict(rows_all=rows_all, q=q, kv_all=kv_all.reshape(2, SLOTS, BLOCK, D), low_all=low_all), rest
 
 
-def tail_back_part(layer, g, r1, r2, acts, slopes, mixed_all, low_all, wo, wes, wrs, g1, g2, outs, scratch):
+def chunk_of(layer, j):
+    return j if layer == 1 else lax.rem(lax.axis_index("dp_0") + 1 + j, STEPS)
+
+
+def tail_back_part(layer, g, r1, r2, acts, slopes, mixed_all, low_all, wo, wes, wrs, g1, g2, outs, scratch, send_chunk=None):
     dwr_out, dwe_out, dwo, gres, gm, vec, vec_e = outs
     dwr, dwe, go, ga, gi, gocat, gacat, gicat, local, send, recv = scratch
     core = lax.axis_index("blk_1")
@@ -858,9 +859,10 @@
     def expand_gradient(j):
         shares[j].wait()
         part = dot_tn(low_all().reshape(2 * ROWS, D), gicat[j].reshape(2 * ROWS, HALF)).astype(BF)
+        at = chunk_of(layer, j)
         for k, piece in enumerate(pieces_of(part)):
-            dwe[k, j] = piece
-        copies.extend(begin([pltpu.make_async_copy(dwe.at[:, j], dwe_out.at[:, j], local.at[1, j])]))
+            dwe[k, at] = piece
+        copies.extend(begin([pltpu.make_async_copy(dwe.at[:, at], dwe_out.at[:, at], local.at[1, j])]))
 
     for j in range(STEPS):
         grad_inner = (dot_nt(go[...], wrs[j]()[...]) * slopes(j).astype(F32)).astype(BF)
@@ -870,18 +872,20 @@
             shares[j].start()
             gicat[j, core] = gi[j, :, mine]
         else:
-            for half in range(2):
-                src = gi.at[j, :, pl.ds(half * HALF, HALF)]
-                dst = dwe_out.at[half, :, pl.ds(j * HALF, HALF)]
-                copies += begin([pltpu.make_async_copy(src, dst, local.at[1 + half, j])])
-        vec_e[:, j * CHUNK : (j + 1) * CHUNK] = jnp.sum(grad_inner.astype(F32), axis=0, keepdims=True)
+            dst = dwe_out.at[core, :, pl.ds(j * HALF, HALF)]
+            copies += begin([pltpu.make_async_copy(gi.at[j, :, mine], dst, local.at[1, j])])
+            copies += begin([remote(gi.at[j, :, yours], dst, send.at[j], recv.at[j], sibling)])
+        at = chunk_of(layer, j)
+        vec_e[:, columns_at(at * CHUNK, CHUNK)] = jnp.sum(grad_inner.astype(F32), axis=0, keepdims=True)
         total = total + dot_nt(grad_inner, wes[j]()[...])
         if j == 0:
             share_go.wait()
         part = dot_tn(acts(j).reshape(2 * ROWS, CHUNK), gocat[...].reshape(2 * ROWS, HALF)).astype(BF)
         for k, piece in enumerate(pieces_of(part)):
-            dwr[k, j] = piece
-        copies += begin([pltpu.make_async_copy(dwr.at[:, j], dwr_out.at[:, j], local.at[0, j])])
+            dwr[k, at] = piece
+        copies += begin([pltpu.make_async_copy(dwr.at[:, at], dwr_out.at[:, at], local.at[0, j])])
+        if send_chunk:
+            send_chunk(j, at, dwr)
         if layer == 0 and j > 0:
             expand_gradient(j - 1)
     normed, inv_std = norm_parts(r1())
@@ -913,32 +917,45 @@
     ]
 
 
-def tail_back_kernel(g, r1, r2, low_all, act_all, slope, mixed_all, wo, we, wr, g1, g2, q_in, e_in, *refs):
+def tail_back_kernel(g, r1, r2, low_all, act_all, slope, mixed_all, wo, we, wr, g1, g2, q_in, *refs):
     refs = list(refs)
 
     def take(count):
         out, refs[:count] = refs[:count], []
         return out
 
-    outs, (got_q, got_e), scratch = take(7), take(2), take(11)
-    held_wr, held_slope, held_we, held_act, held_r1, held_wo, held_mixed, held_low, late, csend, crecv = take(11)
+    outs, (got_q, got_r), scratch = take(7), take(2), take(11)
+    held_wr, held_slope, held_we, held_act, held_r1, held_wo, held_mixed, held_low, late, csend, crecv, rsend, rrecv = take(13)
     core = lax.axis_index("blk_1")
+    met = hail([{"blk_1": 1 - core}] + axis_peers((0, 1, 2)))
     wrs, slopes, wes, acts = [], [], [], []
     for j in range(STEPS):
-        at = chunk_columns(j)
+        at = columns_at(chunk_of(0, j) * CHUNK, CHUNK)
         wrs.append(Late(wr.at[0, at], held_wr.at[j], late.at[4 * j]))
         slopes.append(Late(slope.at[:, at], held_slope.at[j], late.at[4 * j + 1]))
         wes.append(Late(we.at[0, :, at], held_we.at[j], late.at[4 * j + 2]))
-        acts.append(Late(act_all.at[:, j], held_act.at[j], late.at[4 * j + 3]))
+        acts.append(Late(act_all.at[:, chunk_of(0, j)], held_act.at[j], late.at[4 * j + 3]))
     r1, wo = Late(r1, held_r1, late.at[4 * STEPS]), Late(wo.at[0], held_wo, late.at[4 * STEPS + 1])
     mixed_all = Late(mixed_all, held_mixed, late.at[4 * STEPS + 2])
     low_all = Late(low_all, held_low, late.at[4 * STEPS + 3])
-    greet([{"blk_1": 1 - core}] + axis_peers((0, 1, 2)))
-    carried = begin(stage_copies("q", 0, q_in, got_q, csend.at[0], crecv.at[0]))
-    carried += begin(stage_copies("e", 0, e_in, got_e, csend.at[1], crecv.at[1]))
+    met()
+    carried = begin(stage_copies("q", 0, q_in, got_q, csend, crecv))
+    place = chip_place()
+
+    def send_chunk(j, at, dwr):
+        for d in (2, 1, 3):
+            for n, axis in ((0, 2), (1, 1)):
+                to = lax.rem(place[axis] + d, 4)
+                src = dwr.at[0, at, :, lax.rem(to, 2) * 2 + to // 2] if n == 0 else dwr.at[1, at, to]
+                sems = rsend.at[n, d - 1, j], rrecv.at[n, d - 1, j]
+                carried.extend(begin([remote(src, got_r.at[n, d - 1, at], *sems, peer_of(axis, place, d))]))
+        if j < STEPS - 1:
+            sems = rsend.at[2, j, 0], rrecv.at[2, j, 0]
+            carried.extend(begin([remote(dwr.at[2, at], got_r.at[2, j], *sems, peer_of(0, place, j + 1))]))
+
     tail_back_part(
         0, g, lambda: r1()[...], r2, lambda j: acts[j]()[...], lambda j: slopes[j]()[...], lambda: mixed_all()[...],
-        lambda: low_all()[...], wo, wes, wrs, g1, g2, outs, scratch,
+        lambda: low_all()[...], wo, wes, wrs, g1, g2, outs, scratch, send_chunk,
     )
     end(carried)
 
@@ -951,14 +968,14 @@
             shape(WHOLE, BF), shape(WHOLE, BF), shape((D, HALF), BF), shape((ROWS, D), F32), shape((ROWS, D), BF),
             shape((8, D), F32), shape((1, FF), F32), landing(0), landing(0),
         ),
-        in_specs=[VMEM, ANY, VMEM] + [ANY] * 7 + [VMEM, VMEM] + [ANY] * 2,
+        in_specs=[VMEM, ANY, VMEM] + [ANY] * 7 + [VMEM, VMEM, ANY],
         out_specs=(ANY, ANY) + (VMEM,) * 5 + (ANY,) * 2,
         scratch_shapes=tail_back_scratch(0)
         + [
             pltpu.VMEM((STEPS, CHUNK, D), BF), pltpu.VMEM((STEPS, ROWS, CHUNK), BF), pltpu.VMEM((STEPS, D, CHUNK), BF),
             pltpu.VMEM((STEPS, 2, ROWS, CHUNK), BF), pltpu.VMEM((ROWS, D), F32), pltpu.VMEM((D, D), BF),
             pltpu.VMEM((2, ROWS, D), BF), pltpu.VMEM((2, ROWS, D), BF),
-            dma((4 * STEPS + 4,)), dma((2, 3, 3)), dma((2, 3, 3)),
+            dma((4 * STEPS + 4,)), dma((3, 3)), dma((3, 3)), dma((3, 3, STEPS)), dma((3, 3, STEPS)),
         ],
         compiler_params=pltpu.CompilerParams(collective_id=7, has_side_effects=True, vmem_limit_bytes=60 * MIB),
         name="tail_back_0",
@@ -976,44 +993,39 @@
         out, refs[:count] = refs[:count], []
         return out
 
-    rows, gq, parts, gres, dwo, wq, wk, wv = take(8)
-    e0, got_e0, r0, got_r0, q0_two, got_q0_two, e0_two, got_e0_two, r1_two, got_r1_two = take(10)
-    vec_p, vec, vec_e, vec_p_two, vec_two, vec_e_two = take(6)
+    table, (q, kv, gm, rows, gres, dwo, wq, wk, wv, e0, r0, got_r0) = take(4), take(12)
+    q0_two, got_q0_two, e0_two, got_e0_two, r1_two, got_r1_two = take(6)
+    vec, vec_e, vec_p_two, vec_two, vec_e_two = take(5)
     gh, fix_got, rfix_got, v_out = take(4)
-    scratch = take(18)
-    p0, got_q0, own_q0, s_q0, got_q1, s_q1, got_q2 = take(7)
+    held_q, held_kv, held_gm, gq, parts, acc, asems, asend, arecv = take(9)
+    scratch, held = take(9), take(7)
+    p0, got_q0, s_q0, got_q1, s_q1, got_q2 = take(6)
     own_e0, held_e0, s_e0, got_e1, s_e1, got_e2 = take(6)
     own_r0, held_r0, s_r0, got_r1, s_r1, got_r2 = take(6)
     own_q0_two, held_q0_two, s_q0_two, got_q1_two, s_q1_two, got_q2_two = take(6)
     own_e0_two, held_e0_two, s_e0_two, got_e1_two, s_e1_two, got_e2_two = take(6)
     own_r1_two, held_r1_two, s_r1_two, got_r2_two = take(4)
-    fix_send, rfix_send, vsum, vgot, vtotal, vz, vx = take(7)
-    local, send, recv, fsend, frecv, vsend, vrecv = take(7)
+    fix_send, rfix_send, vsum, vgot, vtotal, vz, vx, vec_p, half_got = take(9)
+    local, send, recv, fsend, frecv, vsend, vrecv, hsend, hrecv = take(9)
 
     place = chip_place()
     core = lax.axis_index("blk_1")
     pos = lax.axis_index("dp_2") * 4 + lax.axis_index("blk_0") * 2 + core
     other = 1 - core
     sibling = {"blk_1": other}
-    loads, flights = [], {}
-
-    def start_loads():
-        loads.extend(
-            [
-                begin(own_loads("e", 0, e0, own_e0, got_e0, held_e0, local.at[0])),
-                begin(own_loads("r", 0, r0, own_r0, got_r0, held_r0, local.at[1])),
-                begin(own_loads("q", 0, q0_two, own_q0_two, got_q0_two, held_q0_two, local.at[2])),
-                begin(own_loads("e", 0, e0_two, own_e0_two, got_e0_two, held_e0_two, local.at[3])),
-                begin(own_loads("r", 1, r1_two, own_r1_two, got_r1_two, held_r1_two, local.at[4])),
-            ]
-        )
-        vectors = [vec_p[0:1], vec_p[1:2]] + [vec[k : k + 1] for k in range(6)]
-        vectors += [vec_p_two[0:1], vec_p_two[1:2]] + [vec_two[k : k + 1] for k in range(6)]
-        vectors += [v[:, k * D : (k + 1) * D] for v in (vec_e, vec_e_two) for k in range(4)]
-        for k, vector in enumerate(vectors):
-            vsum[k // 3, k % 3 : k % 3 + 1] = vector
-        for k in range(8):
-            vsum[k, 3:8] = jnp.zeros((5, D), F32)
+    flights = {}
+    met = hail(axis_peers((0, 1)) + [pos_device(lax.rem(pos + d, 8)) for d in range(1, 8)])
+    first = begin(
+        [pltpu.make_async_copy(src, dst, asems.at[n]) for n, (src, dst) in enumerate(((q, held_q), (kv, held_kv), (gm, held_gm)))]
+    )
+    loads = [
+        begin(own_loads("q", 0, q0_two, own_q0_two, got_q0_two, held_q0_two, local.at[0])),
+        begin(own_loads("e", 0, e0_two, own_e0_two, got_e0_two, held_e0_two, local.at[1])),
+        begin(own_loads("r", 1, r1_two, own_r1_two, got_r1_two, held_r1_two, local.at[2])),
+        begin([pltpu.make_async_copy(own_share("e", 0, n, e0), own_e0.at[n], local.at[3, n]) for n in range(3)]),
+        begin(own_loads("r", 0, r0, own_r0, got_r0, held_r0, local.at[4])),
+    ]
+    *weights, rows, gres, dwo = operand_loads(0, wq, wk, wv, rows, gres, dwo, held)
 
     def launch(key, group, stage, source, got, n):
         flights[key] = begin(stage_copies(group, stage, source, got, send.at[n], recv.at[n]))
@@ -1027,24 +1039,6 @@
 
     def along(axis, got, at):
         return begin([remote(vtotal, got.at[d - 1], vsend.at[at + d], vrecv.at[at + d], peer_of(axis, place, d)) for d in (1, 2, 3)])
-
-    def greeted():
-        flights["vc"] = to_all(lambda t: vsum.at[t], vgot, 0)
-        end(loads[0])
-        add_held(own_e0, held_e0, s_e0)
-        launch("e1", "e", 1, s_e0, got_e1, 0)
-        end(loads[1])
-        add_held(own_r0, held_r0, s_r0)
-        launch("r1", "r", 1, s_r0, got_r1, 1)
-        end(loads[2])
-        add_held(own_q0_two, held_q0_two, s_q0_two)
-        launch("q1_two", "q", 1, s_q0_two, got_q1_two, 2)
-        end(loads[3])
-        add_held(own_e0_two, held_e0_two, s_e0_two)
-        launch("e1_two", "e", 1, s_e0_two, got_e1_two, 3)
-        end(loads[4])
-        add_held(own_r1_two, held_r1_two, s_r1_two)
-        launch("r2_two", "r", 2, s_r1_two, got_r2_two, 4)
 
     def far_done():
         end(flights["vc"])
@@ -1074,20 +1068,10 @@
             pl.when(lax.rem(place[2] + d, 4) // 2 == half)(lambda d=d: square_along_y(d).start())
         begin(square_flights(half))
 
-    def two_squares():
-        launch_squares(0)
-
-    def squares():
-        launch_squares(1)
+    def forward_two():
         end(flights["vz"])
         vtotal[...] = vtotal[...] + vz[0] + vz[1] + vz[2]
         flights["vx"] = along(1, vx, 10)
-        end(flights["e1"])
-        add_direct("e", 1, s_e0, got_e1, s_e1)
-        launch("e2", "e", 2, s_e1, got_e2, 7)
-        end(flights["r1"])
-        add_direct("r", 1, s_r0, got_r1, s_r1)
-        launch("r2", "r", 2, s_r1, got_r2, 8)
         end(flights["q1_two"])
         add_direct("q", 1, s_q0_two, got_q1_two, s_q1_two)
         launch("q2_two", "q", 2, s_q1_two, got_q2_two, 6)
@@ -1095,9 +1079,72 @@
         add_direct("e", 1, s_e0_two, got_e1_two, s_e1_two)
         launch("e2_two", "e", 2, s_e1_two, got_e2_two, 11)
 
-    peers = axis_peers((0, 1)) + [pos_device(lax.rem(pos + d, 8)) for d in range(1, 8)]
-    hooks = dict(loads=start_loads, greeted=greeted, far=far_done, two_squares=two_squares, squares=squares)
-    project_back_body(0, rows, gq, parts, gres, dwo, wq, wk, wv, p0, gh, scratch, peers, hooks)
+    met()
+    end(loads[0])
+    add_held(own_q0_two, held_q0_two, s_q0_two)
+    launch("q1_two", "q", 1, s_q0_two, got_q1_two, 2)
+    end(loads[1])
+    add_held(own_e0_two, held_e0_two, s_e0_two)
+    launch("e1_two", "e", 1, s_e0_two, got_e1_two, 3)
+    end(loads[4])
+    add_held(own_r0, held_r0, s_r0)
+    launch("r1", "r", 1, s_r0, got_r1, 1)
+    launch("e0", "e", 0, e0, held_e0, 14)
+    end(loads[2])
+    add_held(own_r1_two, held_r1_two, s_r1_two)
+    launch("r2_two", "r", 2, s_r1_two, got_r2_two, 4)
+    end(first)
+    halves = (half_got, hsend, hrecv)
+    arrived, halves_arrived = attend_back_part(
+        0, table, held_q, held_kv, held_gm, gq, parts, vec_p, acc, scratch[1], None, asend, arecv, halves
+    )
+    vectors = [vec_p[0:1], vec_p[1:2]] + [vec[k : k + 1] for k in range(6)]
+    vectors += [vec_p_two[0:1], vec_p_two[1:2]] + [vec_two[k : k + 1] for k in range(6)]
+    vectors += [v[:, k * D : (k + 1) * D] for v in (vec_e, vec_e_two) for k in range(4)]
+    for k, vector in enumerate(vectors):
+        vsum[k // 3, k % 3 : k % 3 + 1] = vector
+    for k in range(8):
+        vsum[k, 3:8] = jnp.zeros((5, D), F32)
+    flights["vc"] = to_all(lambda t: vsum.at[t], vgot, 0)
+    grads, near, _, gh_send, gh_got, qcat, kvcat, psend, precv = scratch
+    wq, wk, wv = weights
+    y_hi, _, block = places()
+    mine, yours = columns_at(core * HALF, HALF), columns_at(other * HALF, HALF)
+    half_q = remote(gq.at[:, yours], qcat.at[core], psend.at[1], precv.at[1], sibling)
+    half_q.start()
+    qcat[core] = gq[:, mine]
+
+    def place_square(y, grad):
+        for k, piece in enumerate(pieces_of(grad)):
+            p0[k, y] = piece
+
+    place_square(1, dwo()[...])
+    end(halves_arrived)
+    far_at = rows_at(far_start(y_hi), FAR[0])
+    for side in range(2):
+        far = (parts[side, far_at, mine].astype(F32) + half_got[side, 2 * ROWS :].astype(F32)).astype(BF)
+        for c in range(2):
+            here = rows_at((y_hi * 2 + c) * ROWS, ROWS)
+            own = parts[side, here, mine].astype(F32) + half_got[side, c * ROWS : (c + 1) * ROWS].astype(F32)
+            kvcat[side, c, 0:ROWS] = own.astype(BF)
+            kvcat[side, c, ROWS:] = far
+    rows = rows()
+    half_q.wait()
+    place_square(0, (dot_tn(rows[0, 0:ROWS], qcat[0]) + dot_tn(rows[1, 0:ROWS], qcat[1])).astype(BF))
+    launch_squares(0)
+    chip_rows = rows[...].reshape(2 * (ROWS + FAR[0]), D)
+    for side in range(2):
+        place_square(2 + side, dot_tn(chip_rows, kvcat[side].reshape(2 * (ROWS + FAR[0]), HALF)).astype(BF))
+    launch_squares(1)
+    partner, give, theirs = far_plan(0, y_hi, core, block)
+    hidden = remote(gh_send, gh_got, psend.at[0], precv.at[0], partner)
+    wk(), wv()
+
+    @pl.when(is_middle(block))
+    def _():
+        far_k, far_v = parts[0, rows_at(theirs, FAR[0])], parts[1, rows_at(theirs, FAR[0])]
+        gh_send[...] = (dot_nt(far_k, wk()[...]) + dot_nt(far_v, wv()[...])).astype(BF)
+        hidden.start()
 
     def last(group, source, got):
         thirds = []
@@ -1125,46 +1172,66 @@
         sems = fsend.at[layer, 0, 0], frecv.at[layer, 0, 0]
         return begin([remote(rfix_send.at[layer, there], rfix_got.at[layer, core], *sems, sibling)])
 
-    end(flights["vx"])
-    vtotal[...] = vtotal[...] + vx[0] + vx[1] + vx[2]
-    fixes = to_all(lambda t: vtotal, v_out, 13)
-    v_out[pos] = vtotal[...]
+    far_done()
+    end(arrived)
+    grads[:, 0:ROWS] = (parts[:, rows_at(block * ROWS, ROWS)].astype(F32) + near[...].astype(F32)).astype(BF)
+    total = gres()[...] + dot_nt(gq[...], wq()[...])
+    gh[...] = (total + dot_nt(grads[0, 0:ROWS], wk()[...]) + dot_nt(grads[1, 0:ROWS], wv()[...])).astype(BF)
+    end([square_along_y(d) for d in (1, 2, 3)] + square_flights(0) + square_flights(1))
+    add_direct("q", 0, p0, got_q0, s_q0)
+    launch("q1", "q", 1, s_q0, got_q1, 9)
+    end(loads[3] + flights["e0"])
+    add_held(own_e0, held_e0, s_e0)
+    launch("e1", "e", 1, s_e0, got_e1, 0)
+    forward_two()
+    end(flights["r1"])
+    add_direct("r", 1, s_r0, got_r1, s_r1)
+    launch("r2", "r", 2, s_r1, got_r2, 8)
+    end(flights["q1"])
+    add_direct("q", 1, s_q0, got_q1, s_q1)
+    launch("q2", "q", 2, s_q1, got_q2, 10)
+    end(flights["e1"])
+    add_direct("e", 1, s_e0, got_e1, s_e1)
+    launch("e2", "e", 2, s_e1, got_e2, 7)
     end(flights["r2_two"])
-    fixes += reduce_out(1, last("r", s_r1_two, got_r2_two))
-    end(flights["e2"])
-    fixes += rows_out(0, 1, last("e", s_e1, got_e2))
-    end(flights["r2"])
-    fixes += reduce_out(0, last("r", s_r1, got_r2))
+    fixes = reduce_out(1, last("r", s_r1_two, got_r2_two))
     end(flights["q2_two"])
     fixes += rows_out(1, 0, last("q", s_q1_two, got_q2_two))
     end(flights["e2_two"])
     fixes += rows_out(1, 1, last("e", s_e1_two, got_e2_two))
-    for n in range(3):
-        own_q0[n] = own_share("q", 0, n, p0)[...]
-    end([square_along_y(d) for d in (1, 2, 3)] + square_flights(0) + square_flights(1))
-    add_held(own_q0, got_q0, s_q0)
-    launch("q1", "q", 1, s_q0, got_q1, 9)
-    end(flights["q1"])
-    add_direct("q", 1, s_q0, got_q1, s_q1)
-    launch("q2", "q", 2, s_q1, got_q2, 10)
+    end(flights["vx"])
+    vtotal[...] = vtotal[...] + vx[0] + vx[1] + vx[2]
+    fixes += to_all(lambda t: vtotal, v_out, 13)
+    v_out[pos] = vtotal[...]
     end(flights["q2"])
     fixes += rows_out(0, 0, last("q", s_q1, got_q2))
+    end(flights["r2"])
+    fixes += reduce_out(0, last("r", s_r1, got_r2))
+    end(flights["e2"])
+    fixes += rows_out(0, 1, last("e", s_e1, got_e2))
+
+    @pl.when(is_middle(block))
+    def _():
+        hidden.wait()
+        here = rows_at(give, FAR[0])
+        gh[here, :] = (gh[here, :].astype(F32) + gh_got[...].astype(F32)).astype(BF)
+
     for layer in range(2):
         for part in range(2):
             fix_got[layer, part, pos] = fix_send[layer, part, pos]
     end(fixes)
 
 
-def last_step(rows_all, gq, parts, gres, dwo, w, carry, vecs):
+def last_step(table, saved, gm, e0, r0, got_r0, gres, dwo, w, carry, vecs):
     dma, shape = pltpu.SemaphoreType.DMA, jax.ShapeDtypeStruct
     own, got = own_scratch, got_scratch
     return pl.pallas_call(
         last_kernel,
         out_shape=(shape((ROWS, D), BF), shape((2, 2, 8, 8, HALF), F32), shape((2, 2, 24, HALF), F32), shape((8, 8, D), F32)),
-        in_specs=[ANY] * 18 + [VMEM] * 6,
+        in_specs=[SMEM] * 4 + [ANY] * 18 + [VMEM] * 5,
         out_specs=[VMEM] * 4,
-        scratch_shapes=project_back_scratch(0)
-        + [pltpu.VMEM(WHOLE, BF), got(0), own(0), own(0), got(1), own(1), got(2)]
+        scratch_shapes=attend_back_scratch() + project_back_scratch(0) + operand_scratch(0)
+        + [pltpu.VMEM(WHOLE, BF), got(0), own(0), got(1), own(1), got(2)]
         + [own(0), got(0), own(0), got(1), own(1), got(2)] * 4
         + [own(1), got(1), own(1), got(2)]
         + [
@@ -1175,11 +1242,14 @@
             pltpu.VMEM((8, D), F32),
             pltpu.VMEM((3, 8, D), F32),
             pltpu.VMEM((3, 8, D), F32),
-            dma((5, 4)), dma((14, 3, 3)), dma((14, 3, 3)), dma((2, 2, 8)), dma((2, 2, 8)), dma((21,)), dma((21,)),
+            pltpu.VMEM((2, D), F32),
+            pltpu.VMEM((2, 2 * ROWS + FAR[0], HALF), BF),
+            dma((5, 4)), dma((15, 3, 3)), dma((15, 3, 3)), dma((2, 2, 8)), dma((2, 2, 8)), dma((21,)), dma((21,)), dma((2, 3)), dma((2, 3)),
         ],
-        compiler_params=pltpu.CompilerParams(collective_id=3, has_side_effects=True, vmem_limit_bytes=60 * MIB),
+        compiler_params=pltpu.CompilerParams(collective_id=3, has_side_effects=True, vmem_limit_bytes=62 * MIB),
         name="last_step",
-    )(rows_all, gq, parts.reshape(2, SLOTS * BLOCK, D), gres, dwo, w["query_weight"], w["key_weight"], w["value_weight"], *carry, *vecs)
+    )(*table, saved["q"], saved["kv_all"], gm, saved["rows_all"], gres, dwo, w["query_weight"], w["key_weight"], w["value_weight"],
+      e0, r0, got_r0, *carry, *vecs)
 
 
 def finish_kernel(quads, rows, vecs, final, grad, *outs):
@@ -1231,20 +1301,15 @@
 
 def local(hidden, output_grad, block_counts, slot_table, block_order_two, block_order_three, *weights):
     w = dict(zip(NAMES, weights))
-    table = (slot_table, block_counts, block_order_two, block_order_three)
+    table = (slot_table, block_counts, block_order_two.T, block_order_three.T)
     middle, early, saved_one = first_layer(hidden[0], table, w)
     final, saved_two, rest = second_layer(middle, early, output_grad[0], table, w)
     r_two, gi, dwo, gres, gm, vec_two, vec_e_two = rest
-    gq, parts, vec_p_two, gi_other, got_r = attend_back(1, table, saved_two["q"], saved_two["kv_all"], gm, gi, r_two)
-    carry = (gi, gi_other, r_two, got_r)
-    q_two, grad_middle, e_two, r1, got_r = project_back_two(
-        saved_two["rows_all"], gq, parts, gres, dwo, w, saved_two["low_all"], carry
-    )
-    r0, e0, dwo, gres, gm, vec, vec_e, got_q, got_e = tail_back(grad_middle, saved_one, w, (q_two, e_two))
-    gq, parts, vec_p, got_e0, got_r0 = attend_back(0, table, saved_one["q"], saved_one["kv_all"], gm, e0, r0)
-    carry = (e0, got_e0, r0, got_r0, q_two, got_q, e_two, got_e, r1, got_r)
-    vecs = (vec_p, vec, vec_e, vec_p_two, vec_two, vec_e_two)
-    grad_hidden, *sums = last_step(saved_one["rows_all"], gq, parts, gres, dwo, w, carry, vecs)
+    q_two, grad_middle, e_two, r1, got_r, vec_p_two, got_e = second_back(table, saved_two, gm, gi, r_two, gres, dwo, w)
+    r0, e0, dwo, gres, gm, vec, vec_e, got_q, got_r0 = tail_back(grad_middle, saved_one, w, (q_two,))
+    carry = (q_two, got_q, e_two, got_e, r1, got_r)
+    vecs = (vec, vec_e, vec_p_two, vec_two, vec_e_two)
+    grad_hidden, *sums = last_step(table, saved_one, gm, e0, r0, got_r0, gres, dwo, w, carry, vecs)
     return finish(*sums, final, grad_hidden)
 
 

time: 238 us -> 227 us (0.954)
  Pallas kernels: 230 us -> 223 us
  local copies, waits for them, and re-layouts: 2.72 us -> 0 us
    pallas_call x3 -> x1, Pallas kernels: 68.3 us -> 47.2 us  [second_back(): pl.pallas_call(second_back_kernel, out_shape=(shape(WHOLE, BF), shape((RO...]
    pallas_call x1, Pallas kernels: 51.3 us -> 66 us  [last_step(): pl.pallas_call(last_kernel, out_shape=(shape((ROWS, D), BF), shape((2, 2,...]
    pallas_call x1, Pallas kernels: 36.5 us -> 31.5 us  [first_layer(): pl.pallas_call(first_layer_kernel, out_shape=(low, shape((2, SLOTS * BLOC...]
    unnamed x2 -> x0, local copies, waits for them, and re-layouts: 2.72 us -> none
    pallas_call x1, Pallas kernels: 25.9 us -> 28.4 us  [tail_back(): pl.pallas_call(tail_back_kernel, out_shape=(shape(WHOLE, BF), shape(WHOLE...]
where the time goes in v2:
time: 227 us; the launch traced here: 225 us
  Pallas kernels  223 us (98%)
    pallas_call x1, Pallas kernels, last_step(): pl.pallas_call(last_kernel, out_shape=(shape((ROWS, D), BF), shape((2, 2,...  66 us
    pallas_call x1, Pallas kernels, second_back(): pl.pallas_call(second_back_kernel, out_shape=(shape(WHOLE, BF), shape((RO...  47.2 us
    pallas_call x1, Pallas kernels, second_layer(): pl.pallas_call(second_layer_kernel, out_shape=(low, low, shape((2, SLOTS...  47 us
    pallas_call x1, Pallas kernels, first_layer(): pl.pallas_call(first_layer_kernel, out_shape=(low, shape((2, SLOTS * BLOC...  31.5 us
    pallas_call x1, Pallas kernels, tail_back(): pl.pallas_call(tail_back_kernel, out_shape=(shape(WHOLE, BF), shape(WHOLE...  28.4 us

profile of v2, /device:TPU:1, one launch (start us, length us, event | category | flops | bytes accessed | tf_op | source)
XLA Modules:
  0.0 224.5 jit_solution(14702058694592547565)
XLA Ops:
  1.3 31.5 %first_layer.1 = (bf16[384,768]{1,0:T(8,128)(2,1)}, bf16[2,1536,768]{2,1,0:T(8,128)(2,1)}, bf16[2,640,768]{2,1,0:T(8,128)(2,1)}, f32[384,768]{1,0:T(8,128)}, f32...) custom-call(s32[1,3]{1,0:T(1,128)} %refs_0_.1, ...), custom_call_target="tpu_custom_call" | custom-call | tf_op jit(solution)/shard_map/first_layer/pallas_call | solution.py:732
  32.8 47.0 %second_layer.1 = (bf16[384,768]{1,0:T(8,128)(2,1)}, bf16[384,768]{1,0:T(8,128)(2,1)}, bf16[2,1536,768]{2,1,0:T(8,128)(2,1)}, bf16[2,768,768]{2,1,0:T(8,128)(2,1...) custom-call(s32[1,3]{1,0:T(1,128)} %refs_0_.1, ...), custom_call_target="tpu_custom_call" | custom-call | tf_op jit(solution)/shard_map/second_layer/pallas_call | solution.py:816
  79.9 47.2 %second_back.1 = (bf16[3,4,4,4,48,128]{5,4,3,2,1,0:T(8,128)(2,1)}, f32[384,768]{1,0:T(8,128)}, bf16[3,4,4,4,48,128]{5,4,3,2,1,0:T(8,128)(2,1)}, bf16[3,4,4,48,12...) custom-call(s32[1,3]{1,0:T(1,128)} %refs_0_.1, ...), custom_call_target="tpu_custom_call" | custom-call | tf_op jit(solution)/shard_map/second_back/pallas_call | solution.py:392
  127.1 28.4 %tail_back_0.1 = (bf16[3,4,4,4,48,128]{5,4,3,2,1,0:T(8,128)(2,1)}, bf16[3,4,4,4,48,128]{5,4,3,2,1,0:T(8,128)(2,1)}, bf16[768,384]{1,0:T(8,128)(2,1)}, f32[384,76...) custom-call(f32[384,768]{1,0:T(8,128)} %get-tuple-element.90.g, ...), custom_call_target="tpu_custom_call" | custom-call | tf_op jit(solution)/shard_map/tail_back_0/pallas_call | solution.py:965
  155.5 66.0 %last_step.1 = (bf16[384,768]{1,0:T(8,128)(2,1)}, f32[2,2,8,8,384]{4,3,2,1,0:T(8,128)}, f32[2,2,24,384]{3,2,1,0:T(8,128)}, f32[8,8,768]{2,1,0:T(8,128)}) custom-call(s32[1,3]{1,0:T(1,128)} %refs_0_.1, s32[1]{0:T(128)S(6)} %copy.38.cnt.refs_1_, s32[2,12]{1,0:T(2,128)} %bitcast.26, s32[3,12]{1,0:T(4,128)} %bitcast.22, ...), custom_call_target="tpu_custom_call" | custom-call | tf_op jit(solution)/shard_map/last_step/pallas_call | solution.py:1228
  221.5 2.8 %finish.1 = (f32[6,2,768]{2,1,0:T(2,128)}, f32[6,2,768]{2,1,0:T(2,128)}, f32[6,2,768]{2,1,0:T(2,128)}, f32[6,2,768]{2,1,0:T(2,128)}, f32[6,2,3072]{2,1,0:T(2,128...) custom-call(f32[2,2,8,8,384]{4,3,2,1,0:T(8,128)} %get-tuple-element., ...), custom_call_target="tpu_custom_call" | custom-call | tf_op jit(solution)/shard_map/finish/pallas_call | solution.py:1283

commit v3 on v2

--- a/solution.py
+++ b/solution.py
@@ -348,16 +348,16 @@
     core = lax.axis_index("blk_1")
     table = (tab, cnt, two, three)
     met = hail([{"blk_1": 1 - core}] + axis_peers((0, 1, 2)))
-    first = begin(
-        [pltpu.make_async_copy(src, dst, asems.at[n]) for n, (src, dst) in enumerate(((q, held_q), (kv, held_kv), (gm, held_gm)))]
-    )
-    *weights, rows, gres, dwo = operand_loads(1, wq, wk, wv, rows, gres, dwo, held)
     loads = begin(
         [
             pltpu.make_async_copy(gi, gicat, gsems.at[0]),
             pltpu.make_async_copy(low_all, held_low, gsems.at[1]),
         ]
     )
+    first = begin(
+        [pltpu.make_async_copy(src, dst, asems.at[n]) for n, (src, dst) in enumerate(((q, held_q), (kv, held_kv), (gm, held_gm)))]
+    )
+    *weights, rows, gres, dwo = operand_loads(1, wq, wk, wv, rows, gres, dwo, held)
     own_loads_r = begin([pltpu.make_async_copy(own_share("r", 0, n, r0), own_r.at[n], csems.at[n]) for n in range(3)])
     end(loads)
     for y in (0, 2):
@@ -1132,6 +1132,9 @@
     half_q.wait()
     place_square(0, (dot_tn(rows[0, 0:ROWS], qcat[0]) + dot_tn(rows[1, 0:ROWS], qcat[1])).astype(BF))
     launch_squares(0)
+    end(loads[3] + flights["e0"])
+    add_held(own_e0, held_e0, s_e0)
+    launch("e1", "e", 1, s_e0, got_e1, 0)
     chip_rows = rows[...].reshape(2 * (ROWS + FAR[0]), D)
     for side in range(2):
         place_square(2 + side, dot_tn(chip_rows, kvcat[side].reshape(2 * (ROWS + FAR[0]), HALF)).astype(BF))
@@ -1180,9 +1183,9 @@
     end([square_along_y(d) for d in (1, 2, 3)] + square_flights(0) + square_flights(1))
     add_direct("q", 0, p0, got_q0, s_q0)
     launch("q1", "q", 1, s_q0, got_q1, 9)
-    end(loads[3] + flights["e0"])
-    add_held(own_e0, held_e0, s_e0)
-    launch("e1", "e", 1, s_e0, got_e1, 0)
+    end(flights["e1"])
+    add_direct("e", 1, s_e0, got_e1, s_e1)
+    launch("e2", "e", 2, s_e1, got_e2, 7)
     forward_two()
     end(flights["r1"])
     add_direct("r", 1, s_r0, got_r1, s_r1)
@@ -1190,9 +1193,6 @@
     end(flights["q1"])
     add_direct("q", 1, s_q0, got_q1, s_q1)
     launch("q2", "q", 2, s_q1, got_q2, 10)
-    end(flights["e1"])
-    add_direct("e", 1, s_e0, got_e1, s_e1)
-    launch("e2", "e", 2, s_e1, got_e2, 7)
     end(flights["r2_two"])
     fixes = reduce_out(1, last("r", s_r1_two, got_r2_two))
     end(flights["q2_two"])

time: 227 us -> 227 us (level)
  no operation moved by 1% of the time
where the time goes in v3:
time: 227 us; the launch traced here: 224 us
  Pallas kernels  222 us (98%)
    pallas_call x1, Pallas kernels, last_step(): pl.pallas_call(last_kernel, out_shape=(shape((ROWS, D), BF), shape((2, 2,...  65.9 us
    pallas_call x1, Pallas kernels, second_layer(): pl.pallas_call(second_layer_kernel, out_shape=(low, low, shape((2, SLOTS...  47 us
    pallas_call x1, Pallas kernels, second_back(): pl.pallas_call(second_back_kernel, out_shape=(shape(WHOLE, BF), shape((RO...  46.9 us
    pallas_call x1, Pallas kernels, first_layer(): pl.pallas_call(first_layer_kernel, out_shape=(low, shape((2, SLOTS * BLOC...  31.5 us
    pallas_call x1, Pallas kernels, tail_back(): pl.pallas_call(tail_back_kernel, out_shape=(shape(WHOLE, BF), shape(WHOLE...  28.4 us

profile of v3, /device:TPU:1, one launch (start us, length us, event | category | flops | bytes accessed | tf_op | source)
XLA Modules:
  0.0 224.0 jit_solution(9105684048379126605)
XLA Ops:
  1.3 31.5 %first_layer.1 = (bf16[384,768]{1,0:T(8,128)(2,1)}, bf16[2,1536,768]{2,1,0:T(8,128)(2,1)}, bf16[2,640,768]{2,1,0:T(8,128)(2,1)}, f32[384,768]{1,0:T(8,128)}, f32...) custom-call(s32[1,3]{1,0:T(1,128)} %refs_0_.1, ...), custom_call_target="tpu_custom_call" | custom-call | tf_op jit(solution)/shard_map/first_layer/pallas_call | solution.py:732
  32.8 47.0 %second_layer.1 = (bf16[384,768]{1,0:T(8,128)(2,1)}, bf16[384,768]{1,0:T(8,128)(2,1)}, bf16[2,1536,768]{2,1,0:T(8,128)(2,1)}, bf16[2,768,768]{2,1,0:T(8,128)(2,1...) custom-call(s32[1,3]{1,0:T(1,128)} %refs_0_.1, ...), custom_call_target="tpu_custom_call" | custom-call | tf_op jit(solution)/shard_map/second_layer/pallas_call | solution.py:816
  79.9 46.9 %second_back.1 = (bf16[3,4,4,4,48,128]{5,4,3,2,1,0:T(8,128)(2,1)}, f32[384,768]{1,0:T(8,128)}, bf16[3,4,4,4,48,128]{5,4,3,2,1,0:T(8,128)(2,1)}, bf16[3,4,4,48,12...) custom-call(s32[1,3]{1,0:T(1,128)} %refs_0_.1, ...), custom_call_target="tpu_custom_call" | custom-call | tf_op jit(solution)/shard_map/second_back/pallas_call | solution.py:392
  126.8 28.4 %tail_back_0.1 = (bf16[3,4,4,4,48,128]{5,4,3,2,1,0:T(8,128)(2,1)}, bf16[3,4,4,4,48,128]{5,4,3,2,1,0:T(8,128)(2,1)}, bf16[768,384]{1,0:T(8,128)(2,1)}, f32[384,76...) custom-call(f32[384,768]{1,0:T(8,128)} %get-tuple-element.90.g, ...), custom_call_target="tpu_custom_call" | custom-call | tf_op jit(solution)/shard_map/tail_back_0/pallas_call | solution.py:965
  155.2 65.9 %last_step.1 = (bf16[384,768]{1,0:T(8,128)(2,1)}, f32[2,2,8,8,384]{4,3,2,1,0:T(8,128)}, f32[2,2,24,384]{3,2,1,0:T(8,128)}, f32[8,8,768]{2,1,0:T(8,128)}) custom-call(s32[1,3]{1,0:T(1,128)} %refs_0_.1, s32[1]{0:T(128)S(6)} %copy.38.cnt.refs_1_, s32[2,12]{1,0:T(2,128)} %bitcast.26, s32[3,12]{1,0:T(4,128)} %bitcast.22, ...), custom_call_target="tpu_custom_call" | custom-call | tf_op jit(solution)/shard_map/last_step/pallas_call | solution.py:1228
  221.1 2.8 %finish.1 = (f32[6,2,768]{2,1,0:T(2,128)}, f32[6,2,768]{2,1,0:T(2,128)}, f32[6,2,768]{2,1,0:T(2,128)}, f32[6,2,768]{2,1,0:T(2,128)}, f32[6,2,3072]{2,1,0:T(2,128...) custom-call(f32[2,2,8,8,384]{4,3,2,1,0:T(8,128)} %get-tuple-element., ...), custom_call_target="tpu_custom_call" | custom-call | tf_op jit(solution)/shard_map/finish/pallas_call | solution.py:1283
